TPU v7x, 512 devices: a whole 4x8x8 slice. The times are simulated.
512 devices in a mesh: ctx: 64 (over x, z, core), kvh: 8 (over y).
Axes of the slice: x: 4, y: 8, z: 8, core: 2. Of those that a mesh axis runs over, the one named last changes fastest.
Arguments:
- queries: bfloat16 [32768, 64, 128], P('ctx', 'kvh'), may hold values from -5 to 5
- keys: bfloat16 [32768, 8, 128], P('ctx', 'kvh'), may hold values from -5 to 5
- values: bfloat16 [32768, 8, 128], P('ctx', 'kvh'), may hold values from -6 to 6
- doc_ids: int32 [32768], replicated, may hold values from 0 to 31, never falling along the last dimension, each value on 1 to 2560 neighbouring positions
Outputs:
- attended: bfloat16 [32768, 8192], P(('ctx', 'kvh'))
Inputs may be any that keep to these rules, and one draw needn't show every extreme that they name: `doc_ids`: document numbers never fall along the tokens; every document has 1 to 2560 tokens, and one has exactly that many.
All inputs are finite; a program needn't handle non-finite values.
Results may differ from a plain program's by a relative error of at most 0.0037.
Values may be sent and summed in bfloat16 or wider, within the bound.
No kernel may reach another device: no remote copies, remote signals or barrier semaphores. Data moves between devices by JAX's collectives and lax.ppermute only.
A program may use at most 64 MiB of HBM per device.

v0:
```python
import math

import jax
import jax.numpy as jnp
from jax import lax
from jax.sharding import PartitionSpec as P

SPAN = 5


def passed_along(value, axis, steps):
    count = lax.axis_size(axis)
    first, last = (max(0, -steps), min(count, count - steps))
    return lax.ppermute(value, axis, [(source, source + steps) for source in range(first, last)])


def attend_all(query_rows, key_rows, value_rows, allowed_rows, score_scale):
    scores = (
        jnp.einsum("rd,kd->rk", query_rows, key_rows, preferred_element_type=jnp.float32)
        * score_scale
    )
    scores = jnp.where(allowed_rows, scores, -1e30)
    row_max = jnp.max(scores, axis=1, keepdims=True)
    raised = jnp.exp(scores - row_max)
    row_total = jnp.sum(raised, axis=1, keepdims=True)
    weights_bf = raised.astype(jnp.bfloat16)
    weighted = jnp.dot(weights_bf, value_rows, preferred_element_type=jnp.float32) / row_total
    return weighted.astype(jnp.bfloat16)


def on_device(queries, keys, values, doc_ids):
    tok_rows = queries.shape[0]
    kv_dev = keys.shape[1]
    head_dim = keys.shape[2]
    group_size = queries.shape[1] // kv_dev
    score_scale = 1.0 / math.sqrt(head_dim)
    own_index = lax.axis_index("ctx")
    paired = jnp.stack([keys, values], 0)
    moving = paired
    arrived = [paired]
    for distance in range(SPAN):
        moving = passed_along(moving, "ctx", 1)
        arrived.append(moving)
    stacked_kv = jnp.concatenate(arrived[::-1], 1)
    key_width = stacked_kv.shape[1]
    own_start = own_index * tok_rows
    key_pos = own_start - SPAN * tok_rows + jnp.arange(key_width, dtype=jnp.int32)
    padded_docs = jnp.concatenate([jnp.full((SPAN * tok_rows,), -1, jnp.int32), doc_ids])
    key_docs = lax.dynamic_slice_in_dim(padded_docs, own_start, key_width, 0)
    query_docs = lax.dynamic_slice_in_dim(doc_ids, own_start, tok_rows, 0)
    query_pos = own_start + jnp.arange(tok_rows, dtype=jnp.int32)
    allowed = (query_docs[:, None] == key_docs[None, :]) & (key_pos[None, :] <= query_pos[:, None])
    total_rows = tok_rows * group_size
    block_rows = math.gcd(total_rows, 512)
    block_count = total_rows // block_rows
    block_tokens = block_rows // group_size
    flat_rows = queries.reshape(total_rows, head_dim)
    key_rows = stacked_kv[0, :, 0, :]
    value_rows = stacked_kv[1, :, 0, :]

    def one_block(block_index):
        query_rows = lax.dynamic_slice_in_dim(flat_rows, block_index * block_rows, block_rows, 0)
        allowed_rows = lax.dynamic_slice_in_dim(
            allowed, block_index * block_tokens, block_tokens, 0
        )
        allowed_rows = jnp.repeat(allowed_rows, group_size, axis=0)
        return attend_all(query_rows, key_rows, value_rows, allowed_rows, score_scale)

    result = lax.map(one_block, jnp.arange(block_count, dtype=jnp.int32))
    outputs = result.reshape(tok_rows, group_size * head_dim)
    return lax.all_to_all(outputs, "kvh", split_axis=0, concat_axis=1, tiled=True)


def solution(mesh):
    in_specs = (P("ctx", "kvh", None), P("ctx", "kvh", None), P("ctx", "kvh", None), P())
    out_specs = P(("ctx", "kvh"), None)
    return jax.shard_map(
        on_device, mesh=mesh, in_specs=in_specs, out_specs=out_specs, check_vma=False
    )
```

profile of v0, /device:TPU:6, one launch (start us, length us, event | category | flops | bytes accessed | tf_op | source)
XLA Modules:
  0.0 163.0 jit_solution(9831383778746329679)
XLA Ops:
  1.0 1.9 %collective-permute-start = (bf16[2,512,1,128]{3,1,2,0:T(8,128)(2,1)S(1)}, bf16[2,512,1,128]{3,1,2,0:T(8,128)(2,1)S(1)}, u32[]{:S(2)}, u32[]{:S(2)}) collective-permute-start(bf16[2,512,1,128]{3,1,2,0:T(8,128)(2,1)S(1)} %pad_maximum_fusion), channel_id=1, source_target_pairs={{0,8},{8,16},{16,24},{24,32},{32,40},{40,48},{48,56},{56,64},{64,7... | collective-permute-start | bytes 786440 | tf_op jit(solution)/shard_map/ppermute | solution.py:14
  3.0 12.8 %collective-permute-done = bf16[2,512,1,128]{3,1,2,0:T(8,128)(2,1)S(1)} collective-permute-done((bf16[2,512,1,128]{3,1,2,0:T(8,128)(2,1)S(1)}, bf16[2,512,1,128]{3,1,2,0:T(8,128)(2,1)S(1)}, u32[]{:S(2)}, u32[]{:S(2)}) %collective-permute-start) | collective-permute-done | bytes 262176 | tf_op jit(solution)/shard_map/ppermute | solution.py:14
  17.7 7.9 %collective-permute-done.1 = bf16[2,512,1,128]{3,1,2,0:T(8,128)(2,1)S(1)} collective-permute-done((bf16[2,512,1,128]{3,1,2,0:T(8,128)(2,1)S(1)}, bf16[2,512,1,128]{3,1,2,0:T(8,128)(2,1)S(1)}, u32[]{:S(2)}, u32[]{:S(2)}) %collective-permute-start.1) | collective-permute-done | bytes 262176 | tf_op jit(solution)/shard_map/ppermute | solution.py:14
  27.5 7.9 %collective-permute-done.2 = bf16[2,512,1,128]{3,1,2,0:T(8,128)(2,1)S(1)} collective-permute-done((bf16[2,512,1,128]{3,1,2,0:T(8,128)(2,1)S(1)}, bf16[2,512,1,128]{3,1,2,0:T(8,128)(2,1)S(1)}, u32[]{:S(2)}, u32[]{:S(2)}) %collective-permute-start.2) | collective-permute-done | bytes 262176 | tf_op jit(solution)/shard_map/ppermute | solution.py:14
  38.8 6.3 %collective-permute-done.3 = bf16[2,512,1,128]{3,1,2,0:T(8,128)(2,1)S(1)} collective-permute-done((bf16[2,512,1,128]{3,1,2,0:T(8,128)(2,1)S(1)}, bf16[2,512,1,128]{3,1,2,0:T(8,128)(2,1)S(1)}, u32[]{:S(2)}, u32[]{:S(2)}) %collective-permute-start.3) | collective-permute-done | bytes 262176 | tf_op jit(solution)/shard_map/ppermute | solution.py:14
  48.6 6.3 %collective-permute-done.4 = bf16[2,512,1,128]{3,1,2,0:T(8,128)(2,1)S(1)} collective-permute-done((bf16[2,512,1,128]{3,1,2,0:T(8,128)(2,1)S(1)}, bf16[2,512,1,128]{3,1,2,0:T(8,128)(2,1)S(1)}, u32[]{:S(2)}, u32[]{:S(2)}) %collective-permute-start.4) | collective-permute-done | bytes 262176 | tf_op jit(solution)/shard_map/ppermute | solution.py:14
  55.3 75.7 %while.10 = (s32[]{:T(128)}, bf16[8,512,128]{2,1,0:T(8,128)(2,1)}, s32[8]{0:T(128)S(1)}, pred[512,3072]{1,0:T(8,128)(4,1)S(1)}, bf16[4096,128]{1,0:T(8,128)(2,1)...) while((s32[]{:T(128)}, bf16[8,512,128]{2,1,0:T(8,128)(2,1)}, ...), condition=%wide.region_3.4_spmd, body=%wide.region_0.3_spmd.sunk | while | flops 822737920 | bytes 21703404 | solution.py:69
  57.0 2.6 %fusion.34 = (f32[512]{0:T(512)S(1)}, f32[512,3072]{1,0:T(8,128)S(1)}) fusion(pred[64,3072]{1,0:T(8,128)(4,1)S(1)} %constant_dynamic-slice_fusion.2, bf16[3072,128]{1,0:T(8,128)(2,1)S(1)} %get-tuple-element.141, bf16[4096,128]{1,0:T(8,128)(2,1)} %get-tuple-element.140, s32[]{:T(128)S(6)} %select_n.45), kind=kOutput, calls=%fused_computation.2.clone.1 | convolution fusion | flops 407371264 | bytes 7407620 | tf_op jit(solution)/shard_map/while/body/eval_jaxpr/rd,kd->rk/dot_general | solution.py:19
  59.6 2.1 %fusion.35 = f32[512]{0:T(512)S(1)} fusion(f32[512,3072]{1,0:T(8,128)S(1)} %get-tuple-element.108, f32[512]{0:T(512)S(1)} %get-tuple-element.109, pred[64,3072]{1,0:T(8,128)(4,1)S(1)} %constant_dynamic-slice_fusion.2), kind=kLoop, calls=%fused_computation.3.clone.1 | loop fusion | flops 6290944 | bytes 6492160 | tf_op jit(solution)/shard_map/while/body/eval_jaxpr/reduce_sum | solution.py:25
  61.7 3.0 %fusion.36 = bf16[8,512,128]{2,1,0:T(8,128)(2,1)} fusion(bf16[8,512,128]{2,1,0:T(8,128)(2,1)} %get-tuple-element.124, s32[]{:T(128)} %get-tuple-element.123, bf16[3072,128]{1,0:T(8,128)(2,1)S(1)} %get-tuple-element.142, f32[512,3072]{1,0:T(8,128)S(1)} %get-tuple-element.108, f32[512]{0:T(512)S(1)} %get-tuple-element.109, ...), kind=kOutput, calls=%fused_computation.10.clone.1 | convolution fusion | flops 409075712 | bytes 7410176 | tf_op jit(solution)/shard_map/while/body/eval_jaxpr/dot_general | solution.py:27
  66.5 2.6 %fusion.34 = (f32[512]{0:T(512)S(1)}, f32[512,3072]{1,0:T(8,128)S(1)}) fusion(pred[64,3072]{1,0:T(8,128)(4,1)S(1)} %constant_dynamic-slice_fusion.2, bf16[3072,128]{1,0:T(8,128)(2,1)S(1)} %get-tuple-element.141, bf16[4096,128]{1,0:T(8,128)(2,1)} %get-tuple-element.140, s32[]{:T(128)S(6)} %select_n.45), kind=kOutput, calls=%fused_computation.2.clone.1 | convolution fusion | flops 407371264 | bytes 7407620 | tf_op jit(solution)/shard_map/while/body/eval_jaxpr/rd,kd->rk/dot_general | solution.py:19
  69.1 2.1 %fusion.35 = f32[512]{0:T(512)S(1)} fusion(f32[512,3072]{1,0:T(8,128)S(1)} %get-tuple-element.108, f32[512]{0:T(512)S(1)} %get-tuple-element.109, pred[64,3072]{1,0:T(8,128)(4,1)S(1)} %constant_dynamic-slice_fusion.2), kind=kLoop, calls=%fused_computation.3.clone.1 | loop fusion | flops 6290944 | bytes 6492160 | tf_op jit(solution)/shard_map/while/body/eval_jaxpr/reduce_sum | solution.py:25
  71.2 3.0 %fusion.36 = bf16[8,512,128]{2,1,0:T(8,128)(2,1)} fusion(bf16[8,512,128]{2,1,0:T(8,128)(2,1)} %get-tuple-element.124, s32[]{:T(128)} %get-tuple-element.123, bf16[3072,128]{1,0:T(8,128)(2,1)S(1)} %get-tuple-element.142, f32[512,3072]{1,0:T(8,128)S(1)} %get-tuple-element.108, f32[512]{0:T(512)S(1)} %get-tuple-element.109, ...), kind=kOutput, calls=%fused_computation.10.clone.1 | convolution fusion | flops 409075712 | bytes 7410176 | tf_op jit(solution)/shard_map/while/body/eval_jaxpr/dot_general | solution.py:27
  76.0 2.6 %fusion.34 = (f32[512]{0:T(512)S(1)}, f32[512,3072]{1,0:T(8,128)S(1)}) fusion(pred[64,3072]{1,0:T(8,128)(4,1)S(1)} %constant_dynamic-slice_fusion.2, bf16[3072,128]{1,0:T(8,128)(2,1)S(1)} %get-tuple-element.141, bf16[4096,128]{1,0:T(8,128)(2,1)} %get-tuple-element.140, s32[]{:T(128)S(6)} %select_n.45), kind=kOutput, calls=%fused_computation.2.clone.1 | convolution fusion | flops 407371264 | bytes 7407620 | tf_op jit(solution)/shard_map/while/body/eval_jaxpr/rd,kd->rk/dot_general | solution.py:19
  78.6 2.1 %fusion.35 = f32[512]{0:T(512)S(1)} fusion(f32[512,3072]{1,0:T(8,128)S(1)} %get-tuple-element.108, f32[512]{0:T(512)S(1)} %get-tuple-element.109, pred[64,3072]{1,0:T(8,128)(4,1)S(1)} %constant_dynamic-slice_fusion.2), kind=kLoop, calls=%fused_computation.3.clone.1 | loop fusion | flops 6290944 | bytes 6492160 | tf_op jit(solution)/shard_map/while/body/eval_jaxpr/reduce_sum | solution.py:25
  80.7 3.0 %fusion.36 = bf16[8,512,128]{2,1,0:T(8,128)(2,1)} fusion(bf16[8,512,128]{2,1,0:T(8,128)(2,1)} %get-tuple-element.124, s32[]{:T(128)} %get-tuple-element.123, bf16[3072,128]{1,0:T(8,128)(2,1)S(1)} %get-tuple-element.142, f32[512,3072]{1,0:T(8,128)S(1)} %get-tuple-element.108, f32[512]{0:T(512)S(1)} %get-tuple-element.109, ...), kind=kOutput, calls=%fused_computation.10.clone.1 | convolution fusion | flops 409075712 | bytes 7410176 | tf_op jit(solution)/shard_map/while/body/eval_jaxpr/dot_general | solution.py:27
  85.4 2.6 %fusion.34 = (f32[512]{0:T(512)S(1)}, f32[512,3072]{1,0:T(8,128)S(1)}) fusion(pred[64,3072]{1,0:T(8,128)(4,1)S(1)} %constant_dynamic-slice_fusion.2, bf16[3072,128]{1,0:T(8,128)(2,1)S(1)} %get-tuple-element.141, bf16[4096,128]{1,0:T(8,128)(2,1)} %get-tuple-element.140, s32[]{:T(128)S(6)} %select_n.45), kind=kOutput, calls=%fused_computation.2.clone.1 | convolution fusion | flops 407371264 | bytes 7407620 | tf_op jit(solution)/shard_map/while/body/eval_jaxpr/rd,kd->rk/dot_general | solution.py:19
  88.0 2.1 %fusion.35 = f32[512]{0:T(512)S(1)} fusion(f32[512,3072]{1,0:T(8,128)S(1)} %get-tuple-element.108, f32[512]{0:T(512)S(1)} %get-tuple-element.109, pred[64,3072]{1,0:T(8,128)(4,1)S(1)} %constant_dynamic-slice_fusion.2), kind=kLoop, calls=%fused_computation.3.clone.1 | loop fusion | flops 6290944 | bytes 6492160 | tf_op jit(solution)/shard_map/while/body/eval_jaxpr/reduce_sum | solution.py:25
  90.1 3.0 %fusion.36 = bf16[8,512,128]{2,1,0:T(8,128)(2,1)} fusion(bf16[8,512,128]{2,1,0:T(8,128)(2,1)} %get-tuple-element.124, s32[]{:T(128)} %get-tuple-element.123, bf16[3072,128]{1,0:T(8,128)(2,1)S(1)} %get-tuple-element.142, f32[512,3072]{1,0:T(8,128)S(1)} %get-tuple-element.108, f32[512]{0:T(512)S(1)} %get-tuple-element.109, ...), kind=kOutput, calls=%fused_computation.10.clone.1 | convolution fusion | flops 409075712 | bytes 7410176 | tf_op jit(solution)/shard_map/while/body/eval_jaxpr/dot_general | solution.py:27
  94.9 2.6 %fusion.34 = (f32[512]{0:T(512)S(1)}, f32[512,3072]{1,0:T(8,128)S(1)}) fusion(pred[64,3072]{1,0:T(8,128)(4,1)S(1)} %constant_dynamic-slice_fusion.2, bf16[3072,128]{1,0:T(8,128)(2,1)S(1)} %get-tuple-element.141, bf16[4096,128]{1,0:T(8,128)(2,1)} %get-tuple-element.140, s32[]{:T(128)S(6)} %select_n.45), kind=kOutput, calls=%fused_computation.2.clone.1 | convolution fusion | flops 407371264 | bytes 7407620 | tf_op jit(solution)/shard_map/while/body/eval_jaxpr/rd,kd->rk/dot_general | solution.py:19
  97.5 2.1 %fusion.35 = f32[512]{0:T(512)S(1)} fusion(f32[512,3072]{1,0:T(8,128)S(1)} %get-tuple-element.108, f32[512]{0:T(512)S(1)} %get-tuple-element.109, pred[64,3072]{1,0:T(8,128)(4,1)S(1)} %constant_dynamic-slice_fusion.2), kind=kLoop, calls=%fused_computation.3.clone.1 | loop fusion | flops 6290944 | bytes 6492160 | tf_op jit(solution)/shard_map/while/body/eval_jaxpr/reduce_sum | solution.py:25
  99.6 3.0 %fusion.36 = bf16[8,512,128]{2,1,0:T(8,128)(2,1)} fusion(bf16[8,512,128]{2,1,0:T(8,128)(2,1)} %get-tuple-element.124, s32[]{:T(128)} %get-tuple-element.123, bf16[3072,128]{1,0:T(8,128)(2,1)S(1)} %get-tuple-element.142, f32[512,3072]{1,0:T(8,128)S(1)} %get-tuple-element.108, f32[512]{0:T(512)S(1)} %get-tuple-element.109, ...), kind=kOutput, calls=%fused_computation.10.clone.1 | convolution fusion | flops 409075712 | bytes 7410176 | tf_op jit(solution)/shard_map/while/body/eval_jaxpr/dot_general | solution.py:27
  104.4 2.6 %fusion.34 = (f32[512]{0:T(512)S(1)}, f32[512,3072]{1,0:T(8,128)S(1)}) fusion(pred[64,3072]{1,0:T(8,128)(4,1)S(1)} %constant_dynamic-slice_fusion.2, bf16[3072,128]{1,0:T(8,128)(2,1)S(1)} %get-tuple-element.141, bf16[4096,128]{1,0:T(8,128)(2,1)} %get-tuple-element.140, s32[]{:T(128)S(6)} %select_n.45), kind=kOutput, calls=%fused_computation.2.clone.1 | convolution fusion | flops 407371264 | bytes 7407620 | tf_op jit(solution)/shard_map/while/body/eval_jaxpr/rd,kd->rk/dot_general | solution.py:19
  107.0 2.1 %fusion.35 = f32[512]{0:T(512)S(1)} fusion(f32[512,3072]{1,0:T(8,128)S(1)} %get-tuple-element.108, f32[512]{0:T(512)S(1)} %get-tuple-element.109, pred[64,3072]{1,0:T(8,128)(4,1)S(1)} %constant_dynamic-slice_fusion.2), kind=kLoop, calls=%fused_computation.3.clone.1 | loop fusion | flops 6290944 | bytes 6492160 | tf_op jit(solution)/shard_map/while/body/eval_jaxpr/reduce_sum | solution.py:25
  109.1 3.0 %fusion.36 = bf16[8,512,128]{2,1,0:T(8,128)(2,1)} fusion(bf16[8,512,128]{2,1,0:T(8,128)(2,1)} %get-tuple-element.124, s32[]{:T(128)} %get-tuple-element.123, bf16[3072,128]{1,0:T(8,128)(2,1)S(1)} %get-tuple-element.142, f32[512,3072]{1,0:T(8,128)S(1)} %get-tuple-element.108, f32[512]{0:T(512)S(1)} %get-tuple-element.109, ...), kind=kOutput, calls=%fused_computation.10.clone.1 | convolution fusion | flops 409075712 | bytes 7410176 | tf_op jit(solution)/shard_map/while/body/eval_jaxpr/dot_general | solution.py:27
  113.8 2.6 %fusion.34 = (f32[512]{0:T(512)S(1)}, f32[512,3072]{1,0:T(8,128)S(1)}) fusion(pred[64,3072]{1,0:T(8,128)(4,1)S(1)} %constant_dynamic-slice_fusion.2, bf16[3072,128]{1,0:T(8,128)(2,1)S(1)} %get-tuple-element.141, bf16[4096,128]{1,0:T(8,128)(2,1)} %get-tuple-element.140, s32[]{:T(128)S(6)} %select_n.45), kind=kOutput, calls=%fused_computation.2.clone.1 | convolution fusion | flops 407371264 | bytes 7407620 | tf_op jit(solution)/shard_map/while/body/eval_jaxpr/rd,kd->rk/dot_general | solution.py:19
  116.4 2.1 %fusion.35 = f32[512]{0:T(512)S(1)} fusion(f32[512,3072]{1,0:T(8,128)S(1)} %get-tuple-element.108, f32[512]{0:T(512)S(1)} %get-tuple-element.109, pred[64,3072]{1,0:T(8,128)(4,1)S(1)} %constant_dynamic-slice_fusion.2), kind=kLoop, calls=%fused_computation.3.clone.1 | loop fusion | flops 6290944 | bytes 6492160 | tf_op jit(solution)/shard_map/while/body/eval_jaxpr/reduce_sum | solution.py:25
  118.5 3.0 %fusion.36 = bf16[8,512,128]{2,1,0:T(8,128)(2,1)} fusion(bf16[8,512,128]{2,1,0:T(8,128)(2,1)} %get-tuple-element.124, s32[]{:T(128)} %get-tuple-element.123, bf16[3072,128]{1,0:T(8,128)(2,1)S(1)} %get-tuple-element.142, f32[512,3072]{1,0:T(8,128)S(1)} %get-tuple-element.108, f32[512]{0:T(512)S(1)} %get-tuple-element.109, ...), kind=kOutput, calls=%fused_computation.10.clone.1 | convolution fusion | flops 409075712 | bytes 7410176 | tf_op jit(solution)/shard_map/while/body/eval_jaxpr/dot_general | solution.py:27
  123.3 2.6 %fusion.34 = (f32[512]{0:T(512)S(1)}, f32[512,3072]{1,0:T(8,128)S(1)}) fusion(pred[64,3072]{1,0:T(8,128)(4,1)S(1)} %constant_dynamic-slice_fusion.2, bf16[3072,128]{1,0:T(8,128)(2,1)S(1)} %get-tuple-element.141, bf16[4096,128]{1,0:T(8,128)(2,1)} %get-tuple-element.140, s32[]{:T(128)S(6)} %select_n.45), kind=kOutput, calls=%fused_computation.2.clone.1 | convolution fusion | flops 407371264 | bytes 7407620 | tf_op jit(solution)/shard_map/while/body/eval_jaxpr/rd,kd->rk/dot_general | solution.py:19
  125.9 2.1 %fusion.35 = f32[512]{0:T(512)S(1)} fusion(f32[512,3072]{1,0:T(8,128)S(1)} %get-tuple-element.108, f32[512]{0:T(512)S(1)} %get-tuple-element.109, pred[64,3072]{1,0:T(8,128)(4,1)S(1)} %constant_dynamic-slice_fusion.2), kind=kLoop, calls=%fused_computation.3.clone.1 | loop fusion | flops 6290944 | bytes 6492160 | tf_op jit(solution)/shard_map/while/body/eval_jaxpr/reduce_sum | solution.py:25
  128.0 3.0 %fusion.36 = bf16[8,512,128]{2,1,0:T(8,128)(2,1)} fusion(bf16[8,512,128]{2,1,0:T(8,128)(2,1)} %get-tuple-element.124, s32[]{:T(128)} %get-tuple-element.123, bf16[3072,128]{1,0:T(8,128)(2,1)S(1)} %get-tuple-element.142, f32[512,3072]{1,0:T(8,128)S(1)} %get-tuple-element.108, f32[512]{0:T(512)S(1)} %get-tuple-element.109, ...), kind=kOutput, calls=%fused_computation.10.clone.1 | convolution fusion | flops 409075712 | bytes 7410176 | tf_op jit(solution)/shard_map/while/body/eval_jaxpr/dot_general | solution.py:27
  132.6 29.4 %all_to_all.19 = bf16[8,64,1024]{2,1,0:T(8,128)(2,1)S(1)} all-to-all(bf16[8,64,1024]{2,1,0:T(8,128)(2,1)S(1)} %all_to_all.14), channel_id=1, replica_groups=mesh['ctx'=64,'kvh'=8] {'kvh'}, dimensions={0} | all-to-all | bytes 2097152 | tf_op jit(solution)/shard_map/all_to_all | solution.py:71
  (40 shorter events, 19.5 us)
Async XLA Ops:
  0.0 55.1 %copy-start.1 = (bf16[512,1,128]{2,0,1:T(8,128)(2,1)S(1)}, bf16[512,1,128]{2,0,1:T(8,128)(2,1)}, u32[]{:S(2)}) copy-start(bf16[512,1,128]{2,0,1:T(8,128)(2,1)} %param.7) | copy-start | bytes 393220
  0.0 55.1 %copy-start = (bf16[512,1,128]{2,0,1:T(8,128)(2,1)S(1)}, bf16[512,1,128]{2,0,1:T(8,128)(2,1)}, u32[]{:S(2)}) copy-start(bf16[512,1,128]{2,0,1:T(8,128)(2,1)} %param.8) | copy-start | bytes 393220
  1.0 14.7 %collective-permute-start = (bf16[2,512,1,128]{3,1,2,0:T(8,128)(2,1)S(1)}, bf16[2,512,1,128]{3,1,2,0:T(8,128)(2,1)S(1)}, u32[]{:S(2)}, u32[]{:S(2)}) collective-permute-start(bf16[2,512,1,128]{3,1,2,0:T(8,128)(2,1)S(1)} %pad_maximum_fusion), channel_id=1, source_target_pairs={{0,8},{8,16},{16,24},{24,32},{32,40},{40,48},{48,56},{56,64},{64,7... | collective-permute-start | bytes 786440 | tf_op jit(solution)/shard_map/ppermute | solution.py:14
  15.7 9.8 %collective-permute-start.1 = (bf16[2,512,1,128]{3,1,2,0:T(8,128)(2,1)S(1)}, bf16[2,512,1,128]{3,1,2,0:T(8,128)(2,1)S(1)}, u32[]{:S(2)}, u32[]{:S(2)}) collective-permute-start(bf16[2,512,1,128]{3,1,2,0:T(8,128)(2,1)S(1)} %collective-permute-done), channel_id=1, source_target_pairs={{0,8},{8,16},{16,24},{24,32},{32,40},{40,48},{48,56},{56,64},{64,7... | collective-permute-start | bytes 786440 | tf_op jit(solution)/shard_map/ppermute | solution.py:14
  25.5 9.8 %collective-permute-start.2 = (bf16[2,512,1,128]{3,1,2,0:T(8,128)(2,1)S(1)}, bf16[2,512,1,128]{3,1,2,0:T(8,128)(2,1)S(1)}, u32[]{:S(2)}, u32[]{:S(2)}) collective-permute-start(bf16[2,512,1,128]{3,1,2,0:T(8,128)(2,1)S(1)} %collective-permute-done.1), channel_id=1, source_target_pairs={{0,8},{8,16},{16,24},{24,32},{32,40},{40,48},{48,56},{56,64},{64,7... | collective-permute-start | bytes 786440 | tf_op jit(solution)/shard_map/ppermute | solution.py:14
  35.3 9.8 %collective-permute-start.3 = (bf16[2,512,1,128]{3,1,2,0:T(8,128)(2,1)S(1)}, bf16[2,512,1,128]{3,1,2,0:T(8,128)(2,1)S(1)}, u32[]{:S(2)}, u32[]{:S(2)}) collective-permute-start(bf16[2,512,1,128]{3,1,2,0:T(8,128)(2,1)S(1)} %collective-permute-done.2), channel_id=1, source_target_pairs={{0,8},{8,16},{16,24},{24,32},{32,40},{40,48},{48,56},{56,64},{64,7... | collective-permute-start | bytes 786440 | tf_op jit(solution)/shard_map/ppermute | solution.py:14
  45.1 9.8 %collective-permute-start.4 = (bf16[2,512,1,128]{3,1,2,0:T(8,128)(2,1)S(1)}, bf16[2,512,1,128]{3,1,2,0:T(8,128)(2,1)S(1)}, u32[]{:S(2)}, u32[]{:S(2)}) collective-permute-start(bf16[2,512,1,128]{3,1,2,0:T(8,128)(2,1)S(1)} %collective-permute-done.3), channel_id=1, source_target_pairs={{0,8},{8,16},{16,24},{24,32},{32,40},{40,48},{48,56},{56,64},{64,7... | collective-permute-start | bytes 786440 | tf_op jit(solution)/shard_map/ppermute | solution.py:14
where the time goes:
time: 164 us; the launch traced here: 163 us
  matrix products  45 us (27%)
  waiting for transfers between devices  41.1 us (25%)
  blocking collectives  29.4 us (18%)
  other arithmetic  20.3 us (12%)
  starting transfers between devices  9.56 us (6%)
  loops' own time  9.15 us (6%)
  local copies, waits for them, and re-layouts  8.39 us (5%)
    ppermute x5, waiting for transfers between devices, passed_along(): lax.ppermute(value, axis, [(source, source + steps) for source in range(f...  41.1 us
    all_to_all x1, blocking collectives, on_device(): lax.all_to_all(outputs, 'kvh', split_axis=0, concat_axis=1, tiled=True)  29.4 us
    dot_general x8, matrix products, attend_all(): jnp.dot(weights_bf, value_rows, preferred_element_type=jnp.float32)  24.2 us
    dot_general x8, matrix products, attend_all(): jnp.einsum('rd,kd->rk', query_rows, key_rows, preferred_element_type=jnp....  20.8 us
    reduce_sum x8, other arithmetic, attend_all(): row_total = jnp.sum(raised, axis=1, keepdims=True)  16.8 us
    ppermute x5, starting transfers between devices, passed_along(): lax.ppermute(value, axis, [(source, source + steps) for source in range(f...  9.56 us
    another operation x1, loops' own time, on_device(): result = lax.map(one_block, jnp.arange(block_count, dtype=jnp.int32))  9.15 us
    dynamic_slice x8, local copies, waits for them, and re-layouts, on_device(): result = lax.map(one_block, jnp.arange(block_count, dtype=jnp.int32))  4.61 us
  transfers between devices with their start and end apart: 5, of which 5 were waited for; matrix products, arithmetic and copies ran while one was open for 2% of the time, Pallas kernels for 0%

commit v1 on v0

v1 whole, which is shorter than its diff:
```python
import functools
import math

import jax
import jax.numpy as jnp
from jax import lax
from jax.experimental import pallas as pl
from jax.experimental.pallas import tpu as pltpu
from jax.sharding import PartitionSpec as P

SPAN = 5
ONES = 8
COST = 1000
LAG = 3
VMEM = pl.BlockSpec(memory_space=pltpu.VMEM)
SMEM = pl.BlockSpec(memory_space=pltpu.SMEM)
ANY = pl.BlockSpec(memory_space=pl.ANY)
PARAMS = pltpu.CompilerParams(vmem_limit_bytes=32 * 2**20)
bf16, f32, i32 = jnp.bfloat16, jnp.float32, jnp.int32


def hop(value, steps):
    count = lax.axis_size("ctx")
    return lax.ppermute(value, "ctx", [(i, i + steps) for i in range(count - steps)])


def swap_cores(value):
    count = lax.axis_size("ctx")
    return lax.ppermute(value, "ctx", [(i, i ^ 1) for i in range(count)])


def turn(value, steps):
    count = lax.axis_size("kvh")
    return lax.ppermute(value, "kvh", [(i, (i + steps) % count) for i in range(count)])


def values_kernel(kv_ref, out_ref):
    tok = kv_ref.shape[0] // 2
    dim = kv_ref.shape[1]
    out_ref[:dim, :] = kv_ref[tok:, :].T
    out_ref[dim:, :] = jnp.ones((ONES, tok), bf16)


def turned_values(kv):
    tok, dim = kv.shape[0] // 2, kv.shape[1]
    return pl.pallas_call(
        values_kernel,
        in_specs=[VMEM],
        out_specs=VMEM,
        out_shape=jax.ShapeDtypeStruct((dim + ONES, tok), bf16),
        compiler_params=PARAMS,
        cost_estimate=pl.CostEstimate(flops=0, bytes_accessed=4 * tok * dim, transcendentals=0),
        name="values_turned",
    )(kv)


def chunk_kernel(at_ref, qt_ref, first_ref, k_ref, vt_ref, after_ref, other_ref, out_ref, *, tok, heads, part, window):
    chunk = at_ref[0]
    rows = qt_ref.shape[2]
    dim = k_ref.shape[1]
    scale = math.log2(math.e) / math.sqrt(dim)
    base = pl.multiple_of(chunk * part // 128 * 128, 128)
    keys = k_ref[pl.ds(base, window), :]
    scores = jnp.dot(keys, qt_ref[chunk], preferred_element_type=f32) * scale
    first = first_ref[chunk] - base
    own = SPAN * tok + chunk * part - base
    own = own + (lax.broadcasted_iota(i32, (1, rows), 1) & (part - 1))
    key = lax.broadcasted_iota(i32, (window, rows), 0)
    allowed = (key - first).astype(jnp.uint32) <= (own - first).astype(jnp.uint32)
    scores = jnp.where(allowed, scores, -1e30)
    row_max = jnp.max(scores, axis=0, keepdims=True)
    raised = jnp.exp2(scores - row_max)
    total = jnp.dot(
        vt_ref[:, pl.ds(base, window)], raised.astype(bf16), preferred_element_type=f32
    )
    result = (total[:dim] / total[dim : dim + 1]).T.astype(bf16)
    for head in range(heads):
        out_ref[:, head * dim : (head + 1) * dim] = result[head * part : (head + 1) * part]


def attend_chunk(at, qt, first, keys, vt, after, other, tok, heads, part):
    dim = keys.shape[1]
    rows = qt.shape[2]
    window = (SPAN * tok + part + 127) // 128 * 128
    window = window + (128 if part % 128 == 0 else 0)
    window = min(window, keys.shape[0])
    return pl.pallas_call(
        functools.partial(
            chunk_kernel, tok=tok, heads=heads, part=part, window=window
        ),
        in_specs=[SMEM, VMEM, VMEM, VMEM, VMEM, ANY, ANY],
        out_specs=VMEM,
        out_shape=jax.ShapeDtypeStruct((part, heads * dim), bf16),
        compiler_params=PARAMS,
        cost_estimate=pl.CostEstimate(flops=COST, bytes_accessed=0, transcendentals=0),
        name="attend_chunk",
    )(at, qt, first, keys, vt, after, other)


def gather_kernel(source_ref, *refs):
    *pieces, out_ref, sems = refs
    width = pieces[0].shape[1]
    copies = []
    for i, piece in enumerate(pieces):
        place = pl.ds(pl.multiple_of(source_ref[i] * width, 128), width)
        copies.append(pltpu.make_async_copy(piece, out_ref.at[:, place], sems.at[i]))
    for copy in copies:
        copy.start()
    for copy in copies:
        copy.wait()


def gather_pieces(sources, pieces):
    part, width = pieces[0].shape
    count = len(pieces)
    return pl.pallas_call(
        gather_kernel,
        in_specs=[SMEM] + [VMEM] * count,
        out_specs=pl.BlockSpec(memory_space=pl.ANY),
        out_shape=jax.ShapeDtypeStruct((part, count * width), bf16),
        scratch_shapes=[pltpu.SemaphoreType.DMA((count,))],
        compiler_params=PARAMS,
        cost_estimate=pl.CostEstimate(flops=0, bytes_accessed=0, transcendentals=0),
        name="gather_pieces",
    )(sources, *pieces)


def on_device(queries, keys, values, doc_ids):
    tok, heads, dim = queries.shape
    ring = lax.axis_size("kvh")
    part = tok // ring
    me = lax.axis_index("kvh")
    own_index = lax.axis_index("ctx")
    first_core = own_index % 2 == 0

    kv0 = jnp.concatenate([keys[:, 0], values[:, 0]], 0)
    kv2 = hop(kv0, 2)
    kv1 = swap_cores(jnp.where(first_core, kv0, kv2))
    kv4 = hop(kv2, 2)
    kv3 = swap_cores(jnp.where(first_core, kv2, kv4))
    kv5 = hop(kv4, 1)
    blocks = [kv5, kv4, kv3, kv2, kv1, kv0]

    width = (SPAN + 1) * tok
    padded = jnp.concatenate([jnp.full((SPAN * tok,), -1, i32), doc_ids])
    near = lax.dynamic_slice_in_dim(padded, own_index * tok, width, 0)
    mine = near[SPAN * tok :]
    first = jnp.sum((near[None, :] < mine[:, None]).astype(i32), axis=1)
    first = jnp.tile(first.reshape(ring, 1, part), (1, 1, heads))

    qt = queries.reshape(ring, part, heads, dim).transpose(0, 3, 2, 1)
    qt = qt.reshape(ring, dim, heads * part)
    all_keys = jnp.concatenate([b[:tok] for b in blocks], 0)
    vt = jnp.concatenate([turned_values(b) for b in blocks], 1)

    order = (4, 3, 5, 2, 6, 1, 7, 0)
    pieces, piece = [], vt
    for i, steps in enumerate(order):
        at = ((me + steps) % ring).astype(i32).reshape(1)
        other = pieces[i - LAG] if i >= LAG else vt
        piece = attend_chunk(at, qt, first, all_keys, vt, piece, other, tok, heads, part)
        pieces.append(turn(piece, steps) if steps else piece)
    sources = jnp.stack([(me - steps) % ring for steps in order]).astype(i32)
    return gather_pieces(sources, pieces)


def solution(mesh):
    in_specs = (P("ctx", "kvh", None), P("ctx", "kvh", None), P("ctx", "kvh", None), P())
    out_specs = P(("ctx", "kvh"), None)
    return jax.shard_map(
        on_device, mesh=mesh, in_specs=in_specs, out_specs=out_specs, check_vma=False
    )
```

time: 164 us -> 101 us (0.62)
  matrix products: 45 us -> 0 us
  starting transfers between devices: 9.56 us -> 44.3 us
  blocking collectives: 29.4 us -> 0 us
  Pallas kernels: 0 us -> 26.1 us
  waiting for transfers between devices: 41.1 us -> 22 us
  other arithmetic: 20.3 us -> 1.98 us
  loops' own time: 9.15 us -> 0 us
  local copies, waits for them, and re-layouts: 8.39 us -> 4.81 us
    dot_general x16 -> x0, matrix products: 45 us -> none  [the longest x8 24.2 us: attend_all(): jnp.dot(weights_bf, value_rows, preferred_element_type=jnp.float32)]
    ppermute x5 -> x12, starting transfers between devices: 9.56 us -> 44.3 us  [the longest x7 31.9 us: turn(): lax.ppermute(value, 'kvh', [(i, (i + steps) % count) for i in range(count)])]
    all_to_all x1 -> x0, blocking collectives: 29.4 us -> none  [on_device(): lax.all_to_all(outputs, 'kvh', split_axis=0, concat_axis=1, tiled=True)]
    pallas_call x0 -> x15, Pallas kernels: none -> 26.1 us  [the longest x8 23.6 us: attend_chunk(): pl.pallas_call(functools.partial(chunk_kernel, tok=tok, heads=heads, part...]
    ppermute x5 -> x12, waiting for transfers between devices: 41.1 us -> 22 us  [the longest x3 21.2 us: hop(): lax.ppermute(value, 'ctx', [(i, i + steps) for i in range(count - steps)])]
    reduce_sum x8 -> x1, other arithmetic: 16.8 us -> 0.78 us  [on_device(): first = jnp.sum((near[None, :] < mine[:, None]).astype(i32), axis=1)]
    another operation x1 -> x0, loops' own time: 9.15 us -> none  [on_device(): result = lax.map(one_block, jnp.arange(block_count, dtype=jnp.int32))]
    dynamic_slice x17 -> x1, local copies, waits for them, and re-layouts: 5.54 us -> 0.8 us  [on_device(): near = lax.dynamic_slice_in_dim(padded, own_index * tok, width, 0)]
  transfers between devices with their start and end apart: 5 -> 12, of which waited for: 5 -> 3; matrix products, arithmetic and copies ran while one was open for 2% -> 6% of each run, Pallas kernels for 0% -> 21%
where the time goes in v1:
time: 101 us; the launch traced here: 100 us
  starting transfers between devices  44.3 us (44%)
  Pallas kernels  26.1 us (26%)
  waiting for transfers between devices  22 us (22%)
  local copies, waits for them, and re-layouts  4.81 us (5%)
  other arithmetic  1.98 us (2%)
    ppermute x7, starting transfers between devices, turn(): lax.ppermute(value, 'kvh', [(i, (i + steps) % count) for i in range(count)])  31.9 us
    pallas_call x8, Pallas kernels, attend_chunk(): pl.pallas_call(functools.partial(chunk_kernel, tok=tok, heads=heads, part...  23.6 us
    ppermute x3, waiting for transfers between devices, hop(): lax.ppermute(value, 'ctx', [(i, i + steps) for i in range(count - steps)])  21.2 us
    ppermute x3, starting transfers between devices, hop(): lax.ppermute(value, 'ctx', [(i, i + steps) for i in range(count - steps)])  8.1 us
    ppermute x2, starting transfers between devices, swap_cores(): return lax.ppermute(value, 'ctx', [(i, i ^ 1) for i in range(count)])  4.33 us
  transfers between devices with their start and end apart: 12, of which 3 were waited for; matrix products, arithmetic and copies ran while one was open for 6% of the time, Pallas kernels for 21%

profile of v1, /device:TPU:6, one launch (start us, length us, event | category | flops | bytes accessed | tf_op | source)
XLA Modules:
  0.0 100.0 jit_solution(11277966923757438764)
XLA Ops:
  0.0 1.1 %pad_maximum_fusion.kv_ref = bf16[1024,128]{1,0:T(8,128)(2,1)S(1)} fusion(bf16[512,128]{1,0:T(8,128)(2,1)} %bitcast.26, bf16[512,128]{1,0:T(8,128)(2,1)} %bitcast.23), kind=kLoop, calls=%fused_computation.1 | loop fusion | flops 524288 | bytes 524288 | tf_op jit(solution)/shard_map/concatenate | solution.py:136
  1.1 4.3 %collective-permute-start = (bf16[1024,128]{1,0:T(8,128)(2,1)S(1)}, bf16[1024,128]{1,0:T(8,128)(2,1)S(1)}, u32[]{:S(2)}, u32[]{:S(2)}) collective-permute-start(bf16[1024,128]{1,0:T(8,128)(2,1)S(1)} %pad_maximum_fusion.kv_ref), channel_id=1, source_target_pairs={{0,16},{8,24},{16,32},{24,40},{32,48},{40,56},{48,64},{56,72},{64,... | collective-permute-start | bytes 786440 | tf_op jit(solution)/shard_map/ppermute | solution.py:24
  5.4 13.2 %collective-permute-done.kv_ref = bf16[1024,128]{1,0:T(8,128)(2,1)S(1)} collective-permute-done((bf16[1024,128]{1,0:T(8,128)(2,1)S(1)}, bf16[1024,128]{1,0:T(8,128)(2,1)S(1)}, u32[]{:S(2)}, u32[]{:S(2)}) %collective-permute-start) | collective-permute-done | bytes 262176 | tf_op jit(solution)/shard_map/ppermute | solution.py:24
  18.6 1.9 %collective-permute-start.1 = (bf16[1024,128]{1,0:T(8,128)(2,1)S(1)}, bf16[1024,128]{1,0:T(8,128)(2,1)S(1)}, u32[]{:S(2)}, u32[]{:S(2)}) collective-permute-start(bf16[1024,128]{1,0:T(8,128)(2,1)S(1)} %collective-permute-done.kv_ref), channel_id=1, source_target_pairs={{0,16},{8,24},{16,32},{24,40},{32,48},{40,56},{48,64},{56,72},{64,... | collective-permute-start | bytes 786440 | tf_op jit(solution)/shard_map/ppermute | solution.py:24
  20.5 0.8 pad_dynamic-slice_fusion
  21.3 0.8 pad_dynamic-slice_fusion.1
  22.1 8.0 %collective-permute-done.1.kv_ref = bf16[1024,128]{1,0:T(8,128)(2,1)S(1)} collective-permute-done((bf16[1024,128]{1,0:T(8,128)(2,1)S(1)}, bf16[1024,128]{1,0:T(8,128)(2,1)S(1)}, u32[]{:S(2)}, u32[]{:S(2)}) %collective-permute-start.1) | collective-permute-done | bytes 262176 | tf_op jit(solution)/shard_map/ppermute | solution.py:24
  30.1 1.9 %collective-permute-start.2 = (bf16[1024,128]{1,0:T(8,128)(2,1)S(1)}, bf16[1024,128]{1,0:T(8,128)(2,1)S(1)}, u32[]{:S(2)}, u32[]{:S(2)}) collective-permute-start(bf16[1024,128]{1,0:T(8,128)(2,1)S(1)} %collective-permute-done.1.kv_ref), channel_id=1, source_target_pairs={{0,8},{8,16},{16,24},{24,32},{32,40},{40,48},{48,56},{56,64},{64,7... | collective-permute-start | bytes 786440 | tf_op jit(solution)/shard_map/ppermute | solution.py:24
  32.0 0.8 convert_reduce_fusion
  33.0 0.1 tile.12.first_ref
  33.1 1.3 %copy.23 = bf16[8,128,8,64]{1,3,2,0:T(8,128)(2,1)} copy(bf16[8,128,8,64]{1,2,3,0:T(8,128)(2,1)S(1)} %bitcast.25) | data formatting | bytes 2097152 | tf_op jit(solution)/shard_map/transpose | solution.py:151
  34.3 1.5 %copy.24.qt_ref = bf16[8,128,512]{2,1,0:T(8,128)(2,1)S(1)} copy(bf16[8,128,512]{1,2,0:T(8,128)(2,1)} %bitcast.22) | data formatting | bytes 2097152 | tf_op jit(solution)/shard_map/reshape | solution.py:152
  36.0 0.1 broadcast_select_fusion
  36.1 1.9 %collective-permute-start.3 = (bf16[1024,128]{1,0:T(8,128)(2,1)S(1)}, bf16[1024,128]{1,0:T(8,128)(2,1)S(1)}, u32[]{:S(2)}, u32[]{:S(2)}) collective-permute-start(bf16[1024,128]{1,0:T(8,128)(2,1)S(1)} %get-tuple-element.6), channel_id=1, source_target_pairs={{0,8},{8,0},{16,24},{24,16},{32,40},{40,32},{48,56},{56,48},{64,72... | collective-permute-start | bytes 786440 | tf_op jit(solution)/shard_map/ppermute | solution.py:29
  38.0 2.4 %collective-permute-start.4 = (bf16[1024,128]{1,0:T(8,128)(2,1)S(1)}, bf16[1024,128]{1,0:T(8,128)(2,1)S(1)}, u32[]{:S(2)}, u32[]{:S(2)}) collective-permute-start(bf16[1024,128]{1,0:T(8,128)(2,1)S(1)} %get-tuple-element.5), channel_id=1, source_target_pairs={{0,8},{8,0},{16,24},{24,16},{32,40},{40,32},{48,56},{56,48},{64,72... | collective-permute-start | bytes 786440 | tf_op jit(solution)/shard_map/ppermute | solution.py:29
  40.8 0.8 collective-permute-done.4.kv_ref
  41.9 2.6 %attend_chunk.8.after_ref = bf16[64,1024]{1,0:T(8,128)(2,1)S(1)} custom-call(s32[1]{0:T(128)} %bitcast.8.at_ref, bf16[8,128,512]{2,1,0:T(8,128)(2,1)S(1)} %copy.24.qt_ref, s32[8,1,512]{2,1,0:T(1,128)S(1)} %tile.12.first_ref, bf16[3072,128]{1,0:T(8,128)(2,1)S(1)} %constant_dynamic-update-slice_fusion.k_ref, ...), custom_call_target="tpu_custom_call" | custom-call | flops 1000 | tf_op jit(solution)/shard_map/attend_chunk/pallas_call | solution.py:87
  44.6 7.7 %collective-permute-start.5 = (bf16[64,1024]{1,0:T(8,128)(2,1)S(1)}, bf16[64,1024]{1,0:T(8,128)(2,1)S(1)}, u32[]{:S(2)}, u32[]{:S(2)}) collective-permute-start(bf16[64,1024]{1,0:T(8,128)(2,1)S(1)} %attend_chunk.8.after_ref), channel_id=1, source_target_pairs={{0,4},{1,5},{2,6},{3,7},{4,0},{5,1},{6,2},{7,3},{8,12},{9,13},{10,... | collective-permute-start | bytes 393224 | tf_op jit(solution)/shard_map/ppermute | solution.py:34
  52.3 2.6 %attend_chunk.9.after_ref = bf16[64,1024]{1,0:T(8,128)(2,1)S(1)} custom-call(s32[1]{0:T(128)} %bitcast.14.at_ref, bf16[8,128,512]{2,1,0:T(8,128)(2,1)S(1)} %copy.24.qt_ref, s32[8,1,512]{2,1,0:T(1,128)S(1)} %tile.12.first_ref, bf16[3072,128]{1,0:T(8,128)(2,1)S(1)} %constant_dynamic-update-slice_fusion.k_ref, ...), custom_call_target="tpu_custom_call" | custom-call | flops 1000 | tf_op jit(solution)/shard_map/attend_chunk/pallas_call | solution.py:87
  54.9 2.9 %collective-permute-start.6 = (bf16[64,1024]{1,0:T(8,128)(2,1)S(1)}, bf16[64,1024]{1,0:T(8,128)(2,1)S(1)}, u32[]{:S(2)}, u32[]{:S(2)}) collective-permute-start(bf16[64,1024]{1,0:T(8,128)(2,1)S(1)} %attend_chunk.9.after_ref), channel_id=1, source_target_pairs={{0,3},{1,4},{2,5},{3,6},{4,7},{5,0},{6,1},{7,2},{8,11},{9,12},{10,... | collective-permute-start | bytes 393224 | tf_op jit(solution)/shard_map/ppermute | solution.py:34
  57.8 3.3 %attend_chunk.10.after_ref = bf16[64,1024]{1,0:T(8,128)(2,1)} custom-call(s32[1]{0:T(128)} %bitcast.15.at_ref, bf16[8,128,512]{2,1,0:T(8,128)(2,1)S(1)} %copy.24.qt_ref, s32[8,1,512]{2,1,0:T(1,128)S(1)} %tile.12.first_ref, bf16[3072,128]{1,0:T(8,128)(2,1)S(1)} %constant_dynamic-update-slice_fusion.k_ref, ...), custom_call_target="tpu_custom_call" | custom-call | flops 1000 | tf_op jit(solution)/shard_map/attend_chunk/pallas_call | solution.py:87
  61.1 6.1 %collective-permute-start.7 = (bf16[64,1024]{1,0:T(8,128)(2,1)}, bf16[64,1024]{1,0:T(8,128)(2,1)S(1)}, u32[]{:S(2)}, u32[]{:S(2)}) collective-permute-start(bf16[64,1024]{1,0:T(8,128)(2,1)} %attend_chunk.10.after_ref), channel_id=1, source_target_pairs={{0,5},{1,6},{2,7},{3,0},{4,1},{5,2},{6,3},{7,4},{8,13},{9,14},{10,... | collective-permute-start | bytes 393224 | tf_op jit(solution)/shard_map/ppermute | solution.py:34
  67.3 3.3 %attend_chunk.11.after_ref = bf16[64,1024]{1,0:T(8,128)(2,1)} custom-call(s32[1]{0:T(128)} %bitcast.16.at_ref, bf16[8,128,512]{2,1,0:T(8,128)(2,1)S(1)} %copy.24.qt_ref, s32[8,1,512]{2,1,0:T(1,128)S(1)} %tile.12.first_ref, bf16[3072,128]{1,0:T(8,128)(2,1)S(1)} %constant_dynamic-update-slice_fusion.k_ref, ...), custom_call_target="tpu_custom_call" | custom-call | flops 1000 | tf_op jit(solution)/shard_map/attend_chunk/pallas_call | solution.py:87
  70.5 2.7 %collective-permute-start.8 = (bf16[64,1024]{1,0:T(8,128)(2,1)}, bf16[64,1024]{1,0:T(8,128)(2,1)S(1)}, u32[]{:S(2)}, u32[]{:S(2)}) collective-permute-start(bf16[64,1024]{1,0:T(8,128)(2,1)} %attend_chunk.11.after_ref), channel_id=1, source_target_pairs={{0,2},{1,3},{2,4},{3,5},{4,6},{5,7},{6,0},{7,1},{8,10},{9,11},{10,... | collective-permute-start | bytes 393224 | tf_op jit(solution)/shard_map/ppermute | solution.py:34
  73.3 2.6 %attend_chunk.12.after_ref = bf16[64,1024]{1,0:T(8,128)(2,1)S(1)} custom-call(s32[1]{0:T(128)} %bitcast.17.at_ref, bf16[8,128,512]{2,1,0:T(8,128)(2,1)S(1)} %copy.24.qt_ref, s32[8,1,512]{2,1,0:T(1,128)S(1)} %tile.12.first_ref, bf16[3072,128]{1,0:T(8,128)(2,1)S(1)} %constant_dynamic-update-slice_fusion.k_ref, ...), custom_call_target="tpu_custom_call" | custom-call | flops 1000 | tf_op jit(solution)/shard_map/attend_chunk/pallas_call | solution.py:87
  75.9 5.2 %collective-permute-start.9 = (bf16[64,1024]{1,0:T(8,128)(2,1)S(1)}, bf16[64,1024]{1,0:T(8,128)(2,1)S(1)}, u32[]{:S(2)}, u32[]{:S(2)}) collective-permute-start(bf16[64,1024]{1,0:T(8,128)(2,1)S(1)} %attend_chunk.12.after_ref), channel_id=1, source_target_pairs={{0,6},{1,7},{2,0},{3,1},{4,2},{5,3},{6,4},{7,5},{8,14},{9,15},{10,... | collective-permute-start | bytes 393224 | tf_op jit(solution)/shard_map/ppermute | solution.py:34
  81.2 3.2 %attend_chunk.13.after_ref = bf16[64,1024]{1,0:T(8,128)(2,1)} custom-call(s32[1]{0:T(128)} %bitcast.18.at_ref, bf16[8,128,512]{2,1,0:T(8,128)(2,1)S(1)} %copy.24.qt_ref, s32[8,1,512]{2,1,0:T(1,128)S(1)} %tile.12.first_ref, bf16[3072,128]{1,0:T(8,128)(2,1)S(1)} %constant_dynamic-update-slice_fusion.k_ref, ...), custom_call_target="tpu_custom_call" | custom-call | flops 1000 | tf_op jit(solution)/shard_map/attend_chunk/pallas_call | solution.py:87
  84.4 2.5 %collective-permute-start.10 = (bf16[64,1024]{1,0:T(8,128)(2,1)}, bf16[64,1024]{1,0:T(8,128)(2,1)}, u32[]{:S(2)}, u32[]{:S(2)}) collective-permute-start(bf16[64,1024]{1,0:T(8,128)(2,1)} %attend_chunk.13.after_ref), channel_id=1, source_target_pairs={{0,1},{1,2},{2,3},{3,4},{4,5},{5,6},{6,7},{7,0},{8,9},{9,10},{10,1... | collective-permute-start | bytes 393224 | tf_op jit(solution)/shard_map/ppermute | solution.py:34
  86.9 3.3 %attend_chunk.14.after_ref = bf16[64,1024]{1,0:T(8,128)(2,1)} custom-call(s32[1]{0:T(128)} %bitcast.19.at_ref, bf16[8,128,512]{2,1,0:T(8,128)(2,1)S(1)} %copy.24.qt_ref, s32[8,1,512]{2,1,0:T(1,128)S(1)} %tile.12.first_ref, bf16[3072,128]{1,0:T(8,128)(2,1)S(1)} %constant_dynamic-update-slice_fusion.k_ref, ...), custom_call_target="tpu_custom_call" | custom-call | flops 1000 | tf_op jit(solution)/shard_map/attend_chunk/pallas_call | solution.py:87
  90.2 4.7 %collective-permute-start.11 = (bf16[64,1024]{1,0:T(8,128)(2,1)}, bf16[64,1024]{1,0:T(8,128)(2,1)}, u32[]{:S(2)}, u32[]{:S(2)}) collective-permute-start(bf16[64,1024]{1,0:T(8,128)(2,1)} %attend_chunk.14.after_ref), channel_id=1, source_target_pairs={{0,7},{1,0},{2,1},{3,2},{4,3},{5,4},{6,5},{7,6},{8,15},{9,8},{10,9... | collective-permute-start | bytes 393224 | tf_op jit(solution)/shard_map/ppermute | solution.py:34
  95.2 2.6 %attend_chunk.15.refs_7_ = bf16[64,1024]{1,0:T(8,128)(2,1)S(1)} custom-call(s32[1]{0:T(128)} %bitcast.7.at_ref, bf16[8,128,512]{2,1,0:T(8,128)(2,1)S(1)} %copy.24.qt_ref, s32[8,1,512]{2,1,0:T(1,128)S(1)} %tile.12.first_ref, bf16[3072,128]{1,0:T(8,128)(2,1)S(1)} %constant_dynamic-update-slice_fusion.k_ref, ...), custom_call_target="tpu_custom_call" | custom-call | flops 1000 | tf_op jit(solution)/shard_map/attend_chunk/pallas_call | solution.py:87
  97.8 2.0 %gather_pieces.1 = bf16[64,8192]{1,0:T(8,128)(2,1)} custom-call(s32[8]{0:T(128)S(1)} %stack.35.source_ref, bf16[64,1024]{1,0:T(8,128)(2,1)S(1)} %collective-permute-done.5.other_ref.refs_0_, bf16[64,1024]{1,0:T(8,128)(2,1)S(1)} %collective-permute-done.6.other_ref.refs_1_, bf16[64,1024]{1,0:T(8,128)(2,1)S(1)} %collective-permute-done.7.other_ref.refs_2_, ...), custom_call_target="tpu_custom_call" | custom-call | tf_op jit(solution)/shard_map/gather_pieces/pallas_call | solution.py:116
  (36 shorter events, 0.9 us)
Async XLA Ops:
  0.0 33.1 %copy-start.1 = (bf16[512,8,128]{2,1,0:T(8,128)(2,1)S(1)}, bf16[512,8,128]{2,1,0:T(8,128)(2,1)}, u32[]{:S(2)}) copy-start(bf16[512,8,128]{2,1,0:T(8,128)(2,1)} %param.4) | copy-start | bytes 3145732
  1.1 17.5 %collective-permute-start = (bf16[1024,128]{1,0:T(8,128)(2,1)S(1)}, bf16[1024,128]{1,0:T(8,128)(2,1)S(1)}, u32[]{:S(2)}, u32[]{:S(2)}) collective-permute-start(bf16[1024,128]{1,0:T(8,128)(2,1)S(1)} %pad_maximum_fusion.kv_ref), channel_id=1, source_target_pairs={{0,16},{8,24},{16,32},{24,40},{32,48},{40,56},{48,64},{56,72},{64,... | collective-permute-start | bytes 786440 | tf_op jit(solution)/shard_map/ppermute | solution.py:24
  18.6 11.5 %collective-permute-start.1 = (bf16[1024,128]{1,0:T(8,128)(2,1)S(1)}, bf16[1024,128]{1,0:T(8,128)(2,1)S(1)}, u32[]{:S(2)}, u32[]{:S(2)}) collective-permute-start(bf16[1024,128]{1,0:T(8,128)(2,1)S(1)} %collective-permute-done.kv_ref), channel_id=1, source_target_pairs={{0,16},{8,24},{16,32},{24,40},{32,48},{40,56},{48,64},{56,72},{64,... | collective-permute-start | bytes 786440 | tf_op jit(solution)/shard_map/ppermute | solution.py:24
  30.1 10.5 %collective-permute-start.2 = (bf16[1024,128]{1,0:T(8,128)(2,1)S(1)}, bf16[1024,128]{1,0:T(8,128)(2,1)S(1)}, u32[]{:S(2)}, u32[]{:S(2)}) collective-permute-start(bf16[1024,128]{1,0:T(8,128)(2,1)S(1)} %collective-permute-done.1.kv_ref), channel_id=1, source_target_pairs={{0,8},{8,16},{16,24},{24,32},{32,40},{40,48},{48,56},{56,64},{64,7... | collective-permute-start | bytes 786440 | tf_op jit(solution)/shard_map/ppermute | solution.py:24
  34.3 1.6 %copy-start = (bf16[512,1,128]{2,0,1:T(8,128)(2,1)S(1)}, bf16[512,1,128]{2,0,1:T(8,128)(2,1)}, u32[]{:S(2)}) copy-start(bf16[512,1,128]{2,0,1:T(8,128)(2,1)} %param.5) | copy-start | bytes 393220
  34.3 1.6 %copy-start.2 = (bf16[512,1,128]{2,0,1:T(8,128)(2,1)S(1)}, bf16[512,1,128]{2,0,1:T(8,128)(2,1)}, u32[]{:S(2)}) copy-start(bf16[512,1,128]{2,0,1:T(8,128)(2,1)} %param.6) | copy-start | bytes 393220
  36.1 4.6 %collective-permute-start.3 = (bf16[1024,128]{1,0:T(8,128)(2,1)S(1)}, bf16[1024,128]{1,0:T(8,128)(2,1)S(1)}, u32[]{:S(2)}, u32[]{:S(2)}) collective-permute-start(bf16[1024,128]{1,0:T(8,128)(2,1)S(1)} %get-tuple-element.6), channel_id=1, source_target_pairs={{0,8},{8,0},{16,24},{24,16},{32,40},{40,32},{48,56},{56,48},{64,72... | collective-permute-start | bytes 786440 | tf_op jit(solution)/shard_map/ppermute | solution.py:29
  38.0 3.6 %collective-permute-start.4 = (bf16[1024,128]{1,0:T(8,128)(2,1)S(1)}, bf16[1024,128]{1,0:T(8,128)(2,1)S(1)}, u32[]{:S(2)}, u32[]{:S(2)}) collective-permute-start(bf16[1024,128]{1,0:T(8,128)(2,1)S(1)} %get-tuple-element.5), channel_id=1, source_target_pairs={{0,8},{8,0},{16,24},{24,16},{32,40},{40,32},{48,56},{56,48},{64,72... | collective-permute-start | bytes 786440 | tf_op jit(solution)/shard_map/ppermute | solution.py:29
  44.6 22.7 %collective-permute-start.5 = (bf16[64,1024]{1,0:T(8,128)(2,1)S(1)}, bf16[64,1024]{1,0:T(8,128)(2,1)S(1)}, u32[]{:S(2)}, u32[]{:S(2)}) collective-permute-start(bf16[64,1024]{1,0:T(8,128)(2,1)S(1)} %attend_chunk.8.after_ref), channel_id=1, source_target_pairs={{0,4},{1,5},{2,6},{3,7},{4,0},{5,1},{6,2},{7,3},{8,12},{9,13},{10,... | collective-permute-start | bytes 393224 | tf_op jit(solution)/shard_map/ppermute | solution.py:34
  54.9 18.4 %collective-permute-start.6 = (bf16[64,1024]{1,0:T(8,128)(2,1)S(1)}, bf16[64,1024]{1,0:T(8,128)(2,1)S(1)}, u32[]{:S(2)}, u32[]{:S(2)}) collective-permute-start(bf16[64,1024]{1,0:T(8,128)(2,1)S(1)} %attend_chunk.9.after_ref), channel_id=1, source_target_pairs={{0,3},{1,4},{2,5},{3,6},{4,7},{5,0},{6,1},{7,2},{8,11},{9,12},{10,... | collective-permute-start | bytes 393224 | tf_op jit(solution)/shard_map/ppermute | solution.py:34
  61.1 20.0 %collective-permute-start.7 = (bf16[64,1024]{1,0:T(8,128)(2,1)}, bf16[64,1024]{1,0:T(8,128)(2,1)S(1)}, u32[]{:S(2)}, u32[]{:S(2)}) collective-permute-start(bf16[64,1024]{1,0:T(8,128)(2,1)} %attend_chunk.10.after_ref), channel_id=1, source_target_pairs={{0,5},{1,6},{2,7},{3,0},{4,1},{5,2},{6,3},{7,4},{8,13},{9,14},{10,... | collective-permute-start | bytes 393224 | tf_op jit(solution)/shard_map/ppermute | solution.py:34
  70.5 16.4 %collective-permute-start.8 = (bf16[64,1024]{1,0:T(8,128)(2,1)}, bf16[64,1024]{1,0:T(8,128)(2,1)S(1)}, u32[]{:S(2)}, u32[]{:S(2)}) collective-permute-start(bf16[64,1024]{1,0:T(8,128)(2,1)} %attend_chunk.11.after_ref), channel_id=1, source_target_pairs={{0,2},{1,3},{2,4},{3,5},{4,6},{5,7},{6,0},{7,1},{8,10},{9,11},{10,... | collective-permute-start | bytes 393224 | tf_op jit(solution)/shard_map/ppermute | solution.py:34
  75.9 19.2 %collective-permute-start.9 = (bf16[64,1024]{1,0:T(8,128)(2,1)S(1)}, bf16[64,1024]{1,0:T(8,128)(2,1)S(1)}, u32[]{:S(2)}, u32[]{:S(2)}) collective-permute-start(bf16[64,1024]{1,0:T(8,128)(2,1)S(1)} %attend_chunk.12.after_ref), channel_id=1, source_target_pairs={{0,6},{1,7},{2,0},{3,1},{4,2},{5,3},{6,4},{7,5},{8,14},{9,15},{10,... | collective-permute-start | bytes 393224 | tf_op jit(solution)/shard_map/ppermute | solution.py:34
  84.4 13.4 %collective-permute-start.10 = (bf16[64,1024]{1,0:T(8,128)(2,1)}, bf16[64,1024]{1,0:T(8,128)(2,1)}, u32[]{:S(2)}, u32[]{:S(2)}) collective-permute-start(bf16[64,1024]{1,0:T(8,128)(2,1)} %attend_chunk.13.after_ref), channel_id=1, source_target_pairs={{0,1},{1,2},{2,3},{3,4},{4,5},{5,6},{6,7},{7,0},{8,9},{9,10},{10,1... | collective-permute-start | bytes 393224 | tf_op jit(solution)/shard_map/ppermute | solution.py:34
  90.2 7.6 %collective-permute-start.11 = (bf16[64,1024]{1,0:T(8,128)(2,1)}, bf16[64,1024]{1,0:T(8,128)(2,1)}, u32[]{:S(2)}, u32[]{:S(2)}) collective-permute-start(bf16[64,1024]{1,0:T(8,128)(2,1)} %attend_chunk.14.after_ref), channel_id=1, source_target_pairs={{0,7},{1,0},{2,1},{3,2},{4,3},{5,4},{6,5},{7,6},{8,15},{9,8},{10,9... | collective-permute-start | bytes 393224 | tf_op jit(solution)/shard_map/ppermute | solution.py:34

commit v2 on v0

v2 whole, which is shorter than its diff:
```python
import functools
import math

import jax
import jax.numpy as jnp
from jax import lax
from jax.experimental import pallas as pl
from jax.experimental.pallas import tpu as pltpu
from jax.sharding import PartitionSpec as P

SPAN = 5
ONES = 8
COST = 1000
VMEM = pl.BlockSpec(memory_space=pltpu.VMEM)
SMEM = pl.BlockSpec(memory_space=pltpu.SMEM)
ANY = pl.BlockSpec(memory_space=pl.ANY)
PARAMS = pltpu.CompilerParams(vmem_limit_bytes=32 * 2**20)
bf16, f32, i32 = jnp.bfloat16, jnp.float32, jnp.int32


def hop(value, steps):
    count = lax.axis_size("ctx")
    return lax.ppermute(value, "ctx", [(i, i + steps) for i in range(count - steps)])


def swap_cores(value):
    count = lax.axis_size("ctx")
    return lax.ppermute(value, "ctx", [(i, i ^ 1) for i in range(count)])


def scores_of(keys, qt):
    scale = math.log2(math.e) / math.sqrt(keys.shape[1])
    return jnp.dot(keys, qt, preferred_element_type=f32) * scale


def own_kernel(qt_ref, first_ref, kv_ref, acc_ref, max_ref, vt_ref, *, part):
    chunks, dim, rows = qt_ref.shape
    tok = kv_ref.shape[0] // 2
    vt_ref[:dim, :] = kv_ref[tok:, :].T
    vt_ref[dim:, :] = jnp.ones((ONES, tok), bf16)
    place = lax.broadcasted_iota(i32, (1, rows), 1) & (part - 1)
    for chunk in range(chunks):
        width = min(tok, (chunk * part + part + 127) // 128 * 128)
        scores = scores_of(kv_ref[:width, :], qt_ref[chunk])
        first = first_ref[chunk] - SPAN * tok
        own = chunk * part + place
        key = lax.broadcasted_iota(i32, (width, rows), 0)
        scores = jnp.where((key >= first) & (key <= own), scores, -1e30)
        row_max = jnp.max(scores, axis=0, keepdims=True)
        raised = jnp.exp2(scores - row_max).astype(bf16)
        acc_ref[chunk] = jnp.dot(vt_ref[:, :width], raised, preferred_element_type=f32)
        max_ref[chunk] = row_max


def earlier_kernel(ends_ref, qt_ref, first_ref, *refs, base, part, last):
    count = len(refs) - (5 if last else 6)
    blocks, rest = refs[:count], refs[count:]
    if last:
        acc_in, max_in, out_ref, keys_ref, vt_ref = rest
    else:
        acc_in, max_in, acc_out, max_out, keys_ref, vt_ref = rest
    chunks, dim, rows = qt_ref.shape
    tok = blocks[0].shape[0] // 2
    width = count * tok
    for i, block in enumerate(blocks):
        keys_ref[i * tok : (i + 1) * tok, :] = block[:tok, :]
        vt_ref[:dim, i * tok : (i + 1) * tok] = block[tok:, :].T
    vt_ref[dim:, :] = jnp.ones((ONES, width), bf16)

    def step(chunk, masked):
        scores = scores_of(keys_ref[...], qt_ref[chunk])
        if masked:
            key = base + lax.broadcasted_iota(i32, (width, rows), 0)
            scores = jnp.where(key >= first_ref[chunk], scores, -1e30)
        old = max_in[chunk]
        new = jnp.maximum(old, jnp.max(scores, axis=0, keepdims=True))
        raised = jnp.exp2(scores - new).astype(bf16)
        part_sum = jnp.dot(vt_ref[...], raised, preferred_element_type=f32)
        total = acc_in[chunk] * jnp.exp2(old - new) + part_sum
        if last:
            finish(chunk, total)
        else:
            acc_out[chunk] = total
            max_out[chunk] = new

    def finish(chunk, total):
        result = (total[:dim] / total[dim : dim + 1]).T.astype(bf16)
        for head in range(rows // part):
            out_ref[chunk, :, head * dim : (head + 1) * dim] = result[
                head * part : (head + 1) * part
            ]

    def body(chunk, carry):
        whole = base >= ends_ref[1, chunk]
        none = base + width <= ends_ref[0, chunk]

        @pl.when(whole)
        def _():
            step(chunk, False)

        @pl.when(jnp.logical_not(whole | none))
        def _():
            step(chunk, True)

        @pl.when(none)
        def _():
            if last:
                finish(chunk, acc_in[chunk])
            else:
                acc_out[chunk] = acc_in[chunk]
                max_out[chunk] = max_in[chunk]

        return carry

    lax.fori_loop(0, chunks, body, 0)


def attend_own(qt, first, kv, part):
    chunks, dim, rows = qt.shape
    tok = kv.shape[0] // 2
    return pl.pallas_call(
        functools.partial(own_kernel, part=part),
        in_specs=[VMEM] * 3,
        out_specs=[VMEM] * 2,
        out_shape=[
            jax.ShapeDtypeStruct((chunks, dim + ONES, rows), f32),
            jax.ShapeDtypeStruct((chunks, 1, rows), f32),
        ],
        scratch_shapes=[pltpu.VMEM((dim + ONES, tok), bf16)],
        compiler_params=PARAMS,
        cost_estimate=pl.CostEstimate(flops=COST, bytes_accessed=0, transcendentals=0),
        name="attend_own",
    )(qt, first, kv)


def attend_earlier(ends, qt, first, blocks, base, state, part, last=False):
    chunks, dim, rows = qt.shape
    tok = blocks[0].shape[0] // 2
    width = len(blocks) * tok
    acc, row_max = state
    if last:
        out_shape = jax.ShapeDtypeStruct((chunks, part, rows // part * dim), bf16)
        out_specs, alias = VMEM, {}
    else:
        out_shape = [jax.ShapeDtypeStruct(a.shape, f32) for a in state]
        out_specs = [VMEM] * 2
        alias = {3 + len(blocks): 0, 4 + len(blocks): 1}
    return pl.pallas_call(
        functools.partial(earlier_kernel, base=base, part=part, last=last),
        in_specs=[SMEM] + [VMEM] * (4 + len(blocks)),
        out_specs=out_specs,
        out_shape=out_shape,
        input_output_aliases=alias,
        scratch_shapes=[
            pltpu.VMEM((width, dim), bf16),
            pltpu.VMEM((dim + ONES, width), bf16),
        ],
        compiler_params=PARAMS,
        cost_estimate=pl.CostEstimate(flops=COST, bytes_accessed=0, transcendentals=0),
        name="attend_earlier",
    )(ends, qt, first, *blocks, acc, row_max)


def gate(value, after):
    return pl.pallas_call(
        lambda value_ref, after_ref, out_ref: None,
        in_specs=[ANY] * 2,
        out_specs=ANY,
        out_shape=jax.ShapeDtypeStruct(value.shape, value.dtype),
        input_output_aliases={0: 0},
        cost_estimate=pl.CostEstimate(flops=0, bytes_accessed=0, transcendentals=0),
        name="gate",
    )(value, after)


def on_device(queries, keys, values, doc_ids):
    tok, heads, dim = queries.shape
    ring = lax.axis_size("kvh")
    part = tok // ring
    own_index = lax.axis_index("ctx")
    first_core = own_index % 2 == 0

    width = (SPAN + 1) * tok
    padded = jnp.concatenate([jnp.full((SPAN * tok,), -1, i32), doc_ids])
    near = lax.dynamic_slice_in_dim(padded, own_index * tok, width, 0)
    mine = near[SPAN * tok :]
    begins = jnp.sum((near[None, :] < mine[:, None]).astype(i32), axis=1)
    ends = jnp.stack([begins[::part], begins[part - 1 :: part]])
    first = jnp.tile(begins.reshape(ring, 1, part), (1, 1, heads))

    qt = queries.reshape(ring, part, heads, dim).transpose(0, 3, 2, 1)
    qt = qt.reshape(ring, dim, heads * part)

    kv0 = jnp.concatenate([keys[:, 0], values[:, 0]], 0)
    kv2 = hop(kv0, 2)
    state = attend_own(qt, first, kv0, part)
    kv2 = gate(kv2, state[1])
    kv4 = hop(kv2, 2)
    kv1 = swap_cores(jnp.where(first_core, kv0, kv2))
    state = attend_earlier(ends, qt, first, [kv2, kv1], 3 * tok, state, part)
    kv4 = gate(kv4, state[1])
    kv5 = hop(kv4, 1)
    kv3 = swap_cores(jnp.where(first_core, kv2, kv4))
    state = attend_earlier(ends, qt, first, [kv4, kv3], tok, state, part)
    pieces = attend_earlier(ends, qt, first, [kv5], 0, state, part, last=True)
    pieces = lax.all_to_all(pieces, "kvh", split_axis=0, concat_axis=0, tiled=True)
    return pieces.transpose(1, 0, 2).reshape(part, ring * heads * dim)


def solution(mesh):
    in_specs = (P("ctx", "kvh", None), P("ctx", "kvh", None), P("ctx", "kvh", None), P())
    out_specs = P(("ctx", "kvh"), None)
    return jax.shard_map(
        on_device, mesh=mesh, in_specs=in_specs, out_specs=out_specs, check_vma=False
    )
```

time: 164 us -> 94.6 us (0.58)
  the two profiles are of different devices: /device:TPU:6 before, /device:TPU:263 now
where the time goes in v2:
time: 94.6 us; the launch traced here: 93.8 us
  blocking collectives  30 us (32%)
  Pallas kernels  28.7 us (30%)
  starting transfers between devices  14.6 us (15%)
  local copies, waits for them, and re-layouts  14.4 us (15%)
  other arithmetic  5.99 us (6%)
    all_to_all x1, blocking collectives, on_device(): lax.all_to_all(pieces, 'kvh', split_axis=0, concat_axis=0, tiled=True)  30 us
    pallas_call x3, Pallas kernels, attend_earlier(): pl.pallas_call(functools.partial(earlier_kernel, base=base, part=part, la...  24.5 us
    ppermute x3, starting transfers between devices, hop(): lax.ppermute(value, 'ctx', [(i, i + steps) for i in range(count - steps)])  9.88 us
    unnamed x26, local copies, waits for them, and re-layouts  6.85 us
    ppermute x2, starting transfers between devices, swap_cores(): return lax.ppermute(value, 'ctx', [(i, i ^ 1) for i in range(count)])  4.69 us
    pallas_call x1, Pallas kernels, attend_own(): pl.pallas_call(functools.partial(own_kernel, part=part), in_specs=[VMEM]...  4.21 us
    slice x2, local copies, waits for them, and re-layouts, on_device(): ends = jnp.stack([begins[::part], begins[part - 1::part]])  2.67 us
  transfers between devices with their start and end apart: 5, of which 0 were waited for; matrix products, arithmetic and copies ran while one was open for 8% of the time, Pallas kernels for 23%

profile of v2, /device:TPU:263, one launch (start us, length us, event | category | flops | bytes accessed | tf_op | source)
XLA Modules:
  0.0 93.8 jit_solution(15102179859278577952)
XLA Ops:
  0.0 1.7 %pad_maximum_fusion.kv_ref = bf16[1024,128]{1,0:T(8,128)(2,1)} fusion(bf16[512,128]{1,0:T(8,128)(2,1)} %bitcast.14, bf16[512,128]{1,0:T(8,128)(2,1)} %bitcast.16), kind=kLoop, calls=%fused_computation.1 | loop fusion | flops 524288 | bytes 524288 | tf_op jit(solution)/shard_map/concatenate | solution.py:194
  1.7 3.1 %collective-permute-start = (bf16[1024,128]{1,0:T(8,128)(2,1)}, bf16[1024,128]{1,0:T(8,128)(2,1)S(1)}, u32[]{:S(2)}, u32[]{:S(2)}) collective-permute-start(bf16[1024,128]{1,0:T(8,128)(2,1)} %pad_maximum_fusion.kv_ref), channel_id=1, source_target_pairs={{0,16},{8,24},{16,32},{24,40},{32,48},{40,56},{48,64},{56,72},{64,... | collective-permute-start | bytes 786440 | tf_op jit(solution)/shard_map/ppermute | solution.py:23
  4.8 0.8 pad_dynamic-slice_fusion.1
  5.6 0.8 pad_dynamic-slice_fusion
  6.4 0.8 convert_reduce_fusion
  7.2 0.6 copy-done.12
  7.9 1.5 %copy.23 = bf16[8,128,8,64]{1,3,2,0:T(8,128)(2,1)S(1)} copy(bf16[8,128,8,64]{1,2,3,0:T(8,128)(2,1)} %bitcast.13) | data formatting | bytes 2097152 | tf_op jit(solution)/shard_map/transpose | solution.py:191
  9.4 0.5 copy.27.qt_ref
  10.0 4.2 %attend_own.1 = (f32[8,136,512]{2,1,0:T(8,128)S(1)}, f32[8,1,512]{2,1,0:T(1,128)S(1)}) custom-call(bf16[8,128,512]{2,1,0:T(8,128)(2,1)S(1)} %copy.27.qt_ref, s32[8,1,512]{2,1,0:T(1,128)S(1)} %tile.12.first_ref, bf16[1024,128]{1,0:T(8,128)(2,1)} %pad_maximum_fusion.kv_ref), custom_call_target="tpu_custom_call" | custom-call | flops 1000 | tf_op jit(solution)/shard_map/attend_own/pallas_call | solution.py:121
  14.2 0.6 copy-done.3
  14.8 0.7 copy-done
  15.5 1.9 %broadcast_select_fusion.1 = bf16[1024,128]{1,0:T(8,128)(2,1)} fusion(bf16[1024,128]{1,0:T(8,128)(2,1)} %gate.2.refs_0_, pred[]{:T(512)S(6)} %eq.5, bf16[512,128]{1,0:T(8,128)(2,1)} %bitcast.15, bf16[512,128]{1,0:T(8,128)(2,1)} %bitcast.17), kind=kLoop, calls=%fused_computation.3 | loop fusion | flops 655360 | bytes 786433 | tf_op jit(solution)/shard_map/jit(_where)/select_n | solution.py:199
  17.4 2.8 %collective-permute-start.2 = (bf16[1024,128]{1,0:T(8,128)(2,1)}, bf16[1024,128]{1,0:T(8,128)(2,1)}, u32[]{:S(2)}, u32[]{:S(2)}) collective-permute-start(bf16[1024,128]{1,0:T(8,128)(2,1)} %broadcast_select_fusion.1), channel_id=1, source_target_pairs={{0,8},{8,0},{16,24},{24,16},{32,40},{40,32},{48,56},{56,48},{64,72... | collective-permute-start | bytes 786440 | tf_op jit(solution)/shard_map/ppermute | solution.py:28
  20.1 3.1 %collective-permute-start.1 = (bf16[1024,128]{1,0:T(8,128)(2,1)}, bf16[1024,128]{1,0:T(8,128)(2,1)}, u32[]{:S(2)}, u32[]{:S(2)}) collective-permute-start(bf16[1024,128]{1,0:T(8,128)(2,1)} %gate.2.refs_0_), channel_id=1, source_target_pairs={{0,16},{8,24},{16,32},{24,40},{32,48},{40,56},{48,64},{56,72},{64,... | collective-permute-start | bytes 786440 | tf_op jit(solution)/shard_map/ppermute | solution.py:23
  23.3 1.3 %slice.11 = s32[8]{0:T(128)} slice(s32[512]{0:T(512)} %copy-done.12), slice={[63:512:64]} | slice | bytes 64 | tf_op jit(solution)/shard_map/slice | solution.py:188
  24.6 1.3 %slice.10 = s32[8]{0:T(128)} slice(s32[512]{0:T(512)} %copy-done.12), slice={[0:512:64]} | slice | bytes 64 | tf_op jit(solution)/shard_map/slice | solution.py:188
  25.9 0.7 pad_add_fusion.ends_ref
  26.6 0.9 %copy-done.1 = bf16[1024,128]{1,0:T(8,128)(2,1)S(1)} copy-done((bf16[1024,128]{1,0:T(8,128)(2,1)S(1)}, bf16[1024,128]{1,0:T(8,128)(2,1)}, u32[]{:S(2)}) %copy-start.1) | copy-done | bytes 262168
  27.6 0.7 copy-done.4
  28.3 8.8 %attend_earlier.3 = (f32[8,136,512]{2,1,0:T(8,128)S(1)}, f32[8,1,512]{2,1,0:T(1,128)S(1)}) custom-call(s32[2,8]{1,0:T(2,128)S(1)} %pad_add_fusion.ends_ref, bf16[8,128,512]{2,1,0:T(8,128)(2,1)S(1)} %copy.27.qt_ref, s32[8,1,512]{2,1,0:T(1,128)S(1)} %tile.12.first_ref, bf16[1024,128]{1,0:T(8,128)(2,1)S(1)} %copy-done.1, ...), custom_call_target="tpu_custom_call", output_to_operand_aliasing={{0}: (5, {}), {1}: (6, {})} | custom-call | flops 1000 | tf_op jit(solution)/shard_map/attend_earlier/pallas_call | solution.py:148
  37.1 0.6 copy-done.5
  37.7 1.0 %broadcast_select_fusion = bf16[1024,128]{1,0:T(8,128)(2,1)S(1)} fusion(bf16[1024,128]{1,0:T(8,128)(2,1)S(1)} %copy-done.2, bf16[1024,128]{1,0:T(8,128)(2,1)} %gate.3.refs_0_, pred[]{:T(512)S(6)} %eq.5), kind=kLoop, calls=%fused_computation.2 | loop fusion | flops 131072 | bytes 786433 | tf_op jit(solution)/shard_map/jit(_where)/select_n | solution.py:203
  38.7 1.9 %collective-permute-start.4 = (bf16[1024,128]{1,0:T(8,128)(2,1)S(1)}, bf16[1024,128]{1,0:T(8,128)(2,1)S(1)}, u32[]{:S(2)}, u32[]{:S(2)}) collective-permute-start(bf16[1024,128]{1,0:T(8,128)(2,1)S(1)} %broadcast_select_fusion), channel_id=1, source_target_pairs={{0,8},{8,0},{16,24},{24,16},{32,40},{40,32},{48,56},{56,48},{64,72... | collective-permute-start | bytes 786440 | tf_op jit(solution)/shard_map/ppermute | solution.py:28
  40.6 3.7 %collective-permute-start.3 = (bf16[1024,128]{1,0:T(8,128)(2,1)}, bf16[1024,128]{1,0:T(8,128)(2,1)S(1)}, u32[]{:S(2)}, u32[]{:S(2)}) collective-permute-start(bf16[1024,128]{1,0:T(8,128)(2,1)} %gate.3.refs_0_), channel_id=1, source_target_pairs={{0,8},{8,16},{16,24},{24,32},{32,40},{40,48},{48,56},{56,64},{64,7... | collective-permute-start | bytes 786440 | tf_op jit(solution)/shard_map/ppermute | solution.py:23
  44.3 0.7 copy-done.6
  45.0 0.7 copy-done.10
  45.7 8.8 %attend_earlier.4 = (f32[8,136,512]{2,1,0:T(8,128)S(1)}, f32[8,1,512]{2,1,0:T(1,128)S(1)}) custom-call(s32[2,8]{1,0:T(2,128)S(1)} %copy-done.10, bf16[8,128,512]{2,1,0:T(8,128)(2,1)S(1)} %copy.27.qt_ref, s32[8,1,512]{2,1,0:T(1,128)S(1)} %tile.12.first_ref, bf16[1024,128]{1,0:T(8,128)(2,1)} %gate.3.refs_0_, ...), custom_call_target="tpu_custom_call", output_to_operand_aliasing={{0}: (5, {}), {1}: (6, {})} | custom-call | flops 1000 | tf_op jit(solution)/shard_map/attend_earlier/pallas_call | solution.py:148
  54.5 0.6 copy-done.7
  55.1 0.7 copy-done.8
  55.8 6.9 %attend_earlier.5 = bf16[8,64,1024]{2,1,0:T(8,128)(2,1)S(1)} custom-call(s32[2,8]{1,0:T(2,128)S(1)} %copy-done.11, bf16[8,128,512]{2,1,0:T(8,128)(2,1)S(1)} %copy.27.qt_ref, s32[8,1,512]{2,1,0:T(1,128)S(1)} %tile.12.first_ref, bf16[1024,128]{1,0:T(8,128)(2,1)S(1)} %collective-permute-done.3.refs_0_, f32[8,136,512]{2,1,0:T(8,128)S(1)} %get-tuple-element.15.refs_1_, ...), custom_call_target="tpu_custom_call" | custom-call | flops 1000 | tf_op jit(solution)/shard_map/attend_earlier/pallas_call | solution.py:148
  62.7 30.0 %all_to_all.5 = bf16[8,64,1024]{2,1,0:T(8,128)(2,1)S(1)} all-to-all(bf16[8,64,1024]{2,1,0:T(8,128)(2,1)S(1)} %attend_earlier.5), channel_id=1, replica_groups=mesh['ctx'=64,'kvh'=8] {'kvh'}, dimensions={0} | all-to-all | bytes 2097152 | tf_op jit(solution)/shard_map/all_to_all | solution.py:206
  92.7 1.1 %copy.29 = bf16[8,8,8,1024]{3,2,0,1:T(8,128)(2,1)} copy(bf16[8,8,8,1024]{3,2,1,0:T(8,128)(2,1)S(1)} %bitcast.11) | data formatting | bytes 2097152 | tf_op jit(solution)/shard_map/reshape | solution.py:207
  (26 shorter events, 0.2 us)
Async XLA Ops:
  1.7 13.1 %collective-permute-start = (bf16[1024,128]{1,0:T(8,128)(2,1)}, bf16[1024,128]{1,0:T(8,128)(2,1)S(1)}, u32[]{:S(2)}, u32[]{:S(2)}) collective-permute-start(bf16[1024,128]{1,0:T(8,128)(2,1)} %pad_maximum_fusion.kv_ref), channel_id=1, source_target_pairs={{0,16},{8,24},{16,32},{24,40},{32,48},{40,56},{48,64},{56,72},{64,... | collective-permute-start | bytes 786440 | tf_op jit(solution)/shard_map/ppermute | solution.py:23
  7.2 0.6 copy-start.12
  14.2 0.6 copy-start.3
  14.8 0.7 copy-start
  15.5 22.2 %copy-start.2 = (bf16[1024,128]{1,0:T(8,128)(2,1)S(1)}, bf16[1024,128]{1,0:T(8,128)(2,1)}, u32[]{:S(2)}) copy-start(bf16[1024,128]{1,0:T(8,128)(2,1)} %gate.2.refs_0_) | copy-start | bytes 786436
  17.4 9.2 %collective-permute-start.2 = (bf16[1024,128]{1,0:T(8,128)(2,1)}, bf16[1024,128]{1,0:T(8,128)(2,1)}, u32[]{:S(2)}, u32[]{:S(2)}) collective-permute-start(bf16[1024,128]{1,0:T(8,128)(2,1)} %broadcast_select_fusion.1), channel_id=1, source_target_pairs={{0,8},{8,0},{16,24},{24,16},{32,40},{40,32},{48,56},{56,48},{64,72... | collective-permute-start | bytes 786440 | tf_op jit(solution)/shard_map/ppermute | solution.py:28
  20.1 17.5 %collective-permute-start.1 = (bf16[1024,128]{1,0:T(8,128)(2,1)}, bf16[1024,128]{1,0:T(8,128)(2,1)}, u32[]{:S(2)}, u32[]{:S(2)}) collective-permute-start(bf16[1024,128]{1,0:T(8,128)(2,1)} %gate.2.refs_0_), channel_id=1, source_target_pairs={{0,16},{8,24},{16,32},{24,40},{32,48},{40,56},{48,64},{56,72},{64,... | collective-permute-start | bytes 786440 | tf_op jit(solution)/shard_map/ppermute | solution.py:23
  26.6 10.5 %copy-start.9 = (s32[2,8]{1,0:T(2,128)}, s32[2,8]{1,0:T(2,128)S(1)}, u32[]{:S(2)}) copy-start(s32[2,8]{1,0:T(2,128)S(1)} %pad_add_fusion.ends_ref) | copy-start | bytes 196
  26.6 1.0 %copy-start.1 = (bf16[1024,128]{1,0:T(8,128)(2,1)S(1)}, bf16[1024,128]{1,0:T(8,128)(2,1)}, u32[]{:S(2)}) copy-start(bf16[1024,128]{1,0:T(8,128)(2,1)} %gate.2.refs_0_) | copy-start | bytes 786436
  27.6 0.7 copy-start.4
  37.1 0.6 copy-start.5
  37.7 17.4 %copy-start.11 = (s32[2,8]{1,0:T(2,128)S(1)}, s32[2,8]{1,0:T(2,128)}, u32[]{:S(2)}) copy-start(s32[2,8]{1,0:T(2,128)} %copy-done.9) | copy-start | bytes 196
  38.7 5.6 %collective-permute-start.4 = (bf16[1024,128]{1,0:T(8,128)(2,1)S(1)}, bf16[1024,128]{1,0:T(8,128)(2,1)S(1)}, u32[]{:S(2)}, u32[]{:S(2)}) collective-permute-start(bf16[1024,128]{1,0:T(8,128)(2,1)S(1)} %broadcast_select_fusion), channel_id=1, source_target_pairs={{0,8},{8,0},{16,24},{24,16},{32,40},{40,32},{48,56},{56,48},{64,72... | collective-permute-start | bytes 786440 | tf_op jit(solution)/shard_map/ppermute | solution.py:28
  40.6 14.5 %collective-permute-start.3 = (bf16[1024,128]{1,0:T(8,128)(2,1)}, bf16[1024,128]{1,0:T(8,128)(2,1)S(1)}, u32[]{:S(2)}, u32[]{:S(2)}) collective-permute-start(bf16[1024,128]{1,0:T(8,128)(2,1)} %gate.3.refs_0_), channel_id=1, source_target_pairs={{0,8},{8,16},{16,24},{24,32},{32,40},{40,48},{48,56},{56,64},{64,7... | collective-permute-start | bytes 786440 | tf_op jit(solution)/shard_map/ppermute | solution.py:23
  44.3 0.7 copy-start.6
  45.0 0.7 copy-start.10
  54.5 0.6 copy-start.7
  55.1 0.7 copy-start.8

commit v3 on v2

v3 whole, which is shorter than its diff:
```python
import functools
import math

import jax
import jax.numpy as jnp
from jax import lax
from jax.experimental import pallas as pl
from jax.experimental.pallas import tpu as pltpu
from jax.sharding import PartitionSpec as P

SPAN = 5
ONES = 8
ROOM = 100.0
VMEM = pl.BlockSpec(memory_space=pltpu.VMEM)
SMEM = pl.BlockSpec(memory_space=pltpu.SMEM)
ANY = pl.BlockSpec(memory_space=pl.ANY)
PARAMS = pltpu.CompilerParams(vmem_limit_bytes=16 * 2**20)
COST = pl.CostEstimate(flops=1000, bytes_accessed=0, transcendentals=0)
bf16, f32, i32 = jnp.bfloat16, jnp.float32, jnp.int32


def hop(value, steps):
    count = lax.axis_size("ctx")
    return lax.ppermute(value, "ctx", [(i, i + steps) for i in range(count - steps)])


def swap_cores(value):
    count = lax.axis_size("ctx")
    return lax.ppermute(value, "ctx", [(i, i ^ 1) for i in range(count)])


def scores_of(keys, qt):
    scale = math.log2(math.e) / math.sqrt(keys.shape[1])
    return jnp.dot(keys, qt, preferred_element_type=f32) * scale


def own_kernel(qt_ref, first_ref, kv_ref, acc_ref, max_ref, bound_ref, vt_ref, *, part):
    chunks, dim, rows = qt_ref.shape
    tok = kv_ref.shape[0] // 2
    vt_ref[:dim, :] = kv_ref[tok:, :].T
    vt_ref[dim:, :] = jnp.ones((ONES, tok), bf16)
    place = lax.broadcasted_iota(i32, (1, rows), 1) & (part - 1)
    largest = jnp.zeros((1, rows), f32)
    lowest = jnp.full((1, rows), jnp.inf, f32)
    for chunk in range(chunks):
        width = min(tok, (chunk * part + part + 127) // 128 * 128)
        scores = scores_of(kv_ref[:width, :], qt_ref[chunk])
        first = first_ref[chunk] - SPAN * tok
        own = chunk * part + place
        key = lax.broadcasted_iota(i32, (width, rows), 0)
        scores = jnp.where((key >= first) & (key <= own), scores, -1e30)
        row_max = jnp.max(scores, axis=0, keepdims=True)
        raised = jnp.exp2(scores - row_max).astype(bf16)
        acc_ref[chunk] = jnp.dot(vt_ref[:, :width], raised, preferred_element_type=f32)
        max_ref[chunk] = row_max
        squares = jnp.square(qt_ref[chunk].astype(f32))
        largest = jnp.maximum(largest, jnp.sum(squares, axis=0, keepdims=True))
        lowest = jnp.minimum(lowest, row_max)
    bound_ref[0:1] = largest
    bound_ref[1:2] = lowest


def earlier_kernel(qt_ref, first_ref, bound_ref, *refs, base, part, last):
    count = len(refs) - (5 if last else 6)
    blocks, rest = refs[:count], refs[count:]
    if last:
        acc_in, max_in, out_ref, keys_ref, vt_ref = rest
    else:
        acc_in, max_in, acc_out, max_out, keys_ref, vt_ref = rest
    chunks, dim, rows = qt_ref.shape
    tok = blocks[0].shape[0] // 2
    width = count * tok
    end = base + width

    def leave(chunk, total, row_max):
        if last:
            result = (total[:dim] / total[dim : dim + 1]).T.astype(bf16)
            for head in range(rows // part):
                out_ref[chunk, :, head * dim : (head + 1) * dim] = result[
                    head * part : (head + 1) * part
                ]
        else:
            acc_out[chunk] = total
            max_out[chunk] = row_max

    def step(chunk, masked, raising):
        scores = scores_of(keys_ref[...], qt_ref[chunk])
        if masked:
            key = base + lax.broadcasted_iota(i32, (width, rows), 0)
            scores = jnp.where(key >= first_ref[chunk], scores, -1e30)
        old = new = max_in[chunk]
        total = acc_in[chunk]
        if raising:
            new = jnp.maximum(old, jnp.max(scores, axis=0, keepdims=True))
            total = total * jnp.exp2(old - new)
        raised = jnp.exp2(scores - new).astype(bf16)
        total = total + jnp.dot(vt_ref[...], raised, preferred_element_type=f32)
        leave(chunk, total, new)

    lowest_first, highest_first = jnp.min(first_ref[...]), jnp.max(first_ref[...])
    needed = lowest_first < end

    @pl.when(jnp.logical_not(needed))
    def _():
        for chunk in range(chunks):
            leave(chunk, acc_in[chunk], max_in[chunk])

    @pl.when(needed)
    def _():
        for i, block in enumerate(blocks):
            keys_ref[i * tok : (i + 1) * tok, :] = block[:tok, :]
            vt_ref[:dim, i * tok : (i + 1) * tok] = block[tok:, :].T
        vt_ref[dim:, :] = jnp.ones((ONES, width), bf16)
        squares = jnp.square(keys_ref[...].astype(f32))
        key_bound = jnp.max(jnp.sum(squares, axis=1, keepdims=True))
        query_bound = jnp.max(bound_ref[0:1])
        slack = jnp.min(bound_ref[1:2]) + ROOM
        scale = math.log2(math.e) ** 2 / dim * 1.01
        small = (slack > 0) & (query_bound * key_bound * scale <= slack * slack)
        plain = small & (highest_first <= base)

        @pl.when(plain)
        def _():
            for chunk in range(chunks):
                step(chunk, False, False)

        @pl.when(jnp.logical_not(plain))
        def _():
            def body(chunk, carry):
                low, high = jnp.min(first_ref[chunk]), jnp.max(first_ref[chunk])
                some = low < end
                part_of = high > base

                @pl.when(jnp.logical_not(some))
                def _():
                    leave(chunk, acc_in[chunk], max_in[chunk])

                @pl.when(some & small & part_of)
                def _():
                    step(chunk, True, False)

                @pl.when(some & small & jnp.logical_not(part_of))
                def _():
                    step(chunk, False, False)

                @pl.when(some & jnp.logical_not(small))
                def _():
                    step(chunk, True, True)

                return carry

            lax.fori_loop(0, chunks, body, 0)


def attend_own(qt, first, kv, part):
    chunks, dim, rows = qt.shape
    tok = kv.shape[0] // 2
    return pl.pallas_call(
        functools.partial(own_kernel, part=part),
        in_specs=[VMEM] * 3,
        out_specs=[VMEM] * 3,
        out_shape=[
            jax.ShapeDtypeStruct((chunks, dim + ONES, rows), f32),
            jax.ShapeDtypeStruct((chunks, 1, rows), f32),
            jax.ShapeDtypeStruct((2, rows), f32),
        ],
        scratch_shapes=[pltpu.VMEM((dim + ONES, tok), bf16)],
        compiler_params=PARAMS,
        cost_estimate=COST,
        name="attend_own",
    )(qt, first, kv)


def attend_earlier(qt, first, bound, blocks, base, state, part, last=False):
    chunks, dim, rows = qt.shape
    tok = blocks[0].shape[0] // 2
    width = len(blocks) * tok
    acc, row_max = state
    if last:
        out_shape = jax.ShapeDtypeStruct((chunks, part, rows // part * dim), bf16)
        out_specs, alias = VMEM, {}
    else:
        out_shape = [jax.ShapeDtypeStruct(a.shape, f32) for a in state]
        out_specs = [VMEM] * 2
        alias = {3 + len(blocks): 0, 4 + len(blocks): 1}
    return pl.pallas_call(
        functools.partial(earlier_kernel, base=base, part=part, last=last),
        in_specs=[VMEM] * (5 + len(blocks)),
        out_specs=out_specs,
        out_shape=out_shape,
        input_output_aliases=alias,
        scratch_shapes=[
            pltpu.VMEM((width, dim), bf16),
            pltpu.VMEM((dim + ONES, width), bf16),
        ],
        compiler_params=PARAMS,
        cost_estimate=COST,
        name="attend_earlier",
    )(qt, first, bound, *blocks, acc, row_max)


def pass_kernel(second_ref, near_ref, far_ref, after_ref, on_ref, other_ref):
    on_ref[...] = far_ref[...]

    @pl.when(second_ref[0] == 0)
    def _():
        other_ref[...] = near_ref[...]

    @pl.when(second_ref[0] != 0)
    def _():
        other_ref[...] = far_ref[...]


def pass_on(second, near, far, after):
    return pl.pallas_call(
        pass_kernel,
        in_specs=[SMEM, VMEM, VMEM, ANY],
        out_specs=[VMEM] * 2,
        out_shape=[jax.ShapeDtypeStruct(far.shape, far.dtype)] * 2,
        input_output_aliases={2: 0},
        compiler_params=PARAMS,
        cost_estimate=COST,
        name="pass_on",
    )(second, near, far, after)


def on_device(queries, keys, values, doc_ids):
    tok, heads, dim = queries.shape
    ring = lax.axis_size("kvh")
    part = tok // ring
    own_index = lax.axis_index("ctx")
    second = (own_index % 2).astype(i32).reshape(1)

    width = (SPAN + 1) * tok
    padded = jnp.concatenate([jnp.full((SPAN * tok,), -1, i32), doc_ids])
    near = lax.dynamic_slice_in_dim(padded, own_index * tok, width, 0)
    mine = near[SPAN * tok :]
    begins = jnp.sum((near[None, :] < mine[:, None]).astype(i32), axis=1)
    first = jnp.tile(begins.reshape(ring, 1, part), (1, 1, heads))

    qt = queries.reshape(ring, part, heads, dim).transpose(0, 3, 2, 1)
    qt = qt.reshape(ring, dim, heads * part)

    kv0 = jnp.concatenate([keys[:, 0], values[:, 0]], 0)
    kv2 = hop(kv0, 2)
    acc, row_max, bound = attend_own(qt, first, kv0, part)
    kv2, other = pass_on(second, kv0, kv2, row_max)
    kv4 = hop(kv2, 2)
    kv1 = swap_cores(other)
    acc, row_max = attend_earlier(qt, first, bound, [kv2, kv1], 3 * tok, (acc, row_max), part)
    kv4, other = pass_on(second, kv2, kv4, row_max)
    kv5 = hop(kv4, 1)
    kv3 = swap_cores(other)
    acc, row_max = attend_earlier(qt, first, bound, [kv4, kv3], tok, (acc, row_max), part)
    pieces = attend_earlier(qt, first, bound, [kv5], 0, (acc, row_max), part, last=True)
    pieces = lax.all_to_all(pieces, "kvh", split_axis=0, concat_axis=0, tiled=True)
    return pieces.transpose(1, 0, 2).reshape(part, ring * heads * dim)


def solution(mesh):
    in_specs = (P("ctx", "kvh", None), P("ctx", "kvh", None), P("ctx", "kvh", None), P())
    out_specs = P(("ctx", "kvh"), None)
    return jax.shard_map(
        on_device, mesh=mesh, in_specs=in_specs, out_specs=out_specs, check_vma=False
    )
```

time: 94.6 us -> 89.8 us (0.949)
  the two profiles are of different devices: /device:TPU:263 before, /device:TPU:3 now
where the time goes in v3:
time: 89.8 us; the launch traced here: 89.2 us
  blocking collectives  34.7 us (39%)
  Pallas kernels  26.4 us (29%)
  starting transfers between devices  15 us (17%)
  local copies, waits for them, and re-layouts  8.15 us (9%)
  other arithmetic  2.47 us (3%)
  waiting for transfers between devices  2.2 us (2%)
    all_to_all x1, blocking collectives, on_device(): lax.all_to_all(pieces, 'kvh', split_axis=0, concat_axis=0, tiled=True)  34.7 us
    pallas_call x3, Pallas kernels, attend_earlier(): pl.pallas_call(functools.partial(earlier_kernel, base=base, part=part, la...  21.1 us
    ppermute x3, starting transfers between devices, hop(): lax.ppermute(value, 'ctx', [(i, i + steps) for i in range(count - steps)])  9.93 us
    ppermute x2, starting transfers between devices, swap_cores(): return lax.ppermute(value, 'ctx', [(i, i ^ 1) for i in range(count)])  5.05 us
    pallas_call x1, Pallas kernels, attend_own(): pl.pallas_call(functools.partial(own_kernel, part=part), in_specs=[VMEM]...  4.16 us
    unnamed x12, local copies, waits for them, and re-layouts  2.69 us
    ppermute x3, waiting for transfers between devices, hop(): lax.ppermute(value, 'ctx', [(i, i + steps) for i in range(count - steps)])  2.19 us
  transfers between devices with their start and end apart: 5, of which 1 were waited for; matrix products, arithmetic and copies ran while one was open for 6% of the time, Pallas kernels for 28%

profile of v3, /device:TPU:3, one launch (start us, length us, event | category | flops | bytes accessed | tf_op | source)
XLA Modules:
  0.0 89.2 jit_solution(4254599465289533907)
XLA Ops:
  0.0 1.7 %pad_maximum_fusion.kv_ref.near_ref = bf16[1024,128]{1,0:T(8,128)(2,1)} fusion(bf16[512,128]{1,0:T(8,128)(2,1)} %bitcast.13, bf16[512,128]{1,0:T(8,128)(2,1)} %bitcast.14), kind=kLoop, calls=%fused_computation.1 | loop fusion | flops 524288 | bytes 524288 | tf_op jit(solution)/shard_map/concatenate | solution.py:244
  1.7 4.0 %collective-permute-start = (bf16[1024,128]{1,0:T(8,128)(2,1)}, bf16[1024,128]{1,0:T(8,128)(2,1)S(1)}, u32[]{:S(2)}, u32[]{:S(2)}) collective-permute-start(bf16[1024,128]{1,0:T(8,128)(2,1)} %pad_maximum_fusion.kv_ref.near_ref), channel_id=1, source_target_pairs={{0,16},{8,24},{16,32},{24,40},{32,48},{40,56},{48,64},{56,72},{64,... | collective-permute-start | bytes 786440 | tf_op jit(solution)/shard_map/ppermute | solution.py:24
  5.7 0.8 pad_dynamic-slice_fusion.1
  6.5 0.8 pad_dynamic-slice_fusion
  7.3 0.8 convert_reduce_fusion
  8.1 0.1 tile.10
  8.1 0.7 tile.12.first_ref
  8.8 1.5 %copy.23 = bf16[8,128,8,64]{1,3,2,0:T(8,128)(2,1)S(1)} copy(bf16[8,128,8,64]{1,2,3,0:T(8,128)(2,1)} %bitcast.12) | data formatting | bytes 2097152 | tf_op jit(solution)/shard_map/transpose | solution.py:241
  10.3 0.5 copy.27.qt_ref
  10.9 0.7 copy-done
  11.6 4.2 %attend_own.1 = (f32[8,136,512]{2,1,0:T(8,128)S(1)}, f32[8,1,512]{2,1,0:T(1,128)S(1)}, f32[2,512]{1,0:T(2,128)S(1)}) custom-call(bf16[8,128,512]{2,1,0:T(8,128)(2,1)S(1)} %copy.27.qt_ref, s32[8,1,512]{2,1,0:T(1,128)S(1)} %copy-done, bf16[1024,128]{1,0:T(8,128)(2,1)} %pad_maximum_fusion.kv_ref.near_ref), custom_call_target="tpu_custom_call" | custom-call | flops 1000 | tf_op jit(solution)/shard_map/attend_own/pallas_call | solution.py:158
  15.8 0.0 copy-start.3
  15.8 0.6 copy-done.3
  16.4 2.2 %collective-permute-done.far_ref = bf16[1024,128]{1,0:T(8,128)(2,1)S(1)} collective-permute-done((bf16[1024,128]{1,0:T(8,128)(2,1)}, bf16[1024,128]{1,0:T(8,128)(2,1)S(1)}, u32[]{:S(2)}, u32[]{:S(2)}) %collective-permute-start) | collective-permute-done | bytes 262176 | tf_op jit(solution)/shard_map/ppermute | solution.py:24
  18.6 1.0 %pass_on.2 = (bf16[1024,128]{1,0:T(8,128)(2,1)S(1)}, bf16[1024,128]{1,0:T(8,128)(2,1)S(1)}) custom-call(s32[1]{0:T(128)} %bitcast.5.second_ref, bf16[1024,128]{1,0:T(8,128)(2,1)} %pad_maximum_fusion.kv_ref.near_ref, bf16[1024,128]{1,0:T(8,128)(2,1)S(1)} %collective-permute-done.far_ref, ...), custom_call_target="tpu_custom_call", output_to_operand_aliasing={{0}: (2, {})} | custom-call | flops 1000 | tf_op jit(solution)/shard_map/pass_on/pallas_call | solution.py:215
  19.6 3.1 %collective-permute-start.2 = (bf16[1024,128]{1,0:T(8,128)(2,1)S(1)}, bf16[1024,128]{1,0:T(8,128)(2,1)S(1)}, u32[]{:S(2)}, u32[]{:S(2)}) collective-permute-start(bf16[1024,128]{1,0:T(8,128)(2,1)S(1)} %get-tuple-element.19), channel_id=1, source_target_pairs={{0,8},{8,0},{16,24},{24,16},{32,40},{40,32},{48,56},{56,48},{64,72... | collective-permute-start | bytes 786440 | tf_op jit(solution)/shard_map/ppermute | solution.py:29
  22.7 1.9 %collective-permute-start.1 = (bf16[1024,128]{1,0:T(8,128)(2,1)S(1)}, bf16[1024,128]{1,0:T(8,128)(2,1)S(1)}, u32[]{:S(2)}, u32[]{:S(2)}) collective-permute-start(bf16[1024,128]{1,0:T(8,128)(2,1)S(1)} %get-tuple-element.18.refs_0_.near_ref), channel_id=1, source_target_pairs={{0,16},{8,24},{16,32},{24,40},{32,48},{40,56},{48,64},{56,72},{64,... | collective-permute-start | bytes 786440 | tf_op jit(solution)/shard_map/ppermute | solution.py:24
  24.7 0.0 collective-permute-done.2.refs_1_
  24.7 0.7 copy-done.1
  25.4 0.7 copy-done.4
  26.1 10.0 %attend_earlier.3 = (f32[8,136,512]{2,1,0:T(8,128)S(1)}, f32[8,1,512]{2,1,0:T(1,128)S(1)}) custom-call(bf16[8,128,512]{2,1,0:T(8,128)(2,1)S(1)} %copy.27.qt_ref, s32[8,1,512]{2,1,0:T(1,128)S(1)} %copy-done.1, f32[2,512]{1,0:T(2,128)S(1)} %copy-done.4, ...), custom_call_target="tpu_custom_call", output_to_operand_aliasing={{0}: (5, {}), {1}: (6, {})} | custom-call | flops 1000 | tf_op jit(solution)/shard_map/attend_earlier/pallas_call | solution.py:186
  36.1 0.0 collective-permute-done.1.far_ref
  36.1 0.1 pass_on.3
  36.2 1.9 %collective-permute-start.4 = (bf16[1024,128]{1,0:T(8,128)(2,1)S(1)}, bf16[1024,128]{1,0:T(8,128)(2,1)S(1)}, u32[]{:S(2)}, u32[]{:S(2)}) collective-permute-start(bf16[1024,128]{1,0:T(8,128)(2,1)S(1)} %get-tuple-element.23), channel_id=1, source_target_pairs={{0,8},{8,0},{16,24},{24,16},{32,40},{40,32},{48,56},{56,48},{64,72... | collective-permute-start | bytes 786440 | tf_op jit(solution)/shard_map/ppermute | solution.py:29
  38.2 4.0 %collective-permute-start.3 = (bf16[1024,128]{1,0:T(8,128)(2,1)S(1)}, bf16[1024,128]{1,0:T(8,128)(2,1)S(1)}, u32[]{:S(2)}, u32[]{:S(2)}) collective-permute-start(bf16[1024,128]{1,0:T(8,128)(2,1)S(1)} %get-tuple-element.22.refs_0_), channel_id=1, source_target_pairs={{0,8},{8,16},{16,24},{24,32},{32,40},{40,48},{48,56},{56,64},{64,7... | collective-permute-start | bytes 786440 | tf_op jit(solution)/shard_map/ppermute | solution.py:24
  42.2 0.0 collective-permute-done.4.refs_1_
  42.2 0.0 copy-done.5
  42.2 10.5 %attend_earlier.4 = (f32[8,136,512]{2,1,0:T(8,128)S(1)}, f32[8,1,512]{2,1,0:T(1,128)S(1)}) custom-call(bf16[8,128,512]{2,1,0:T(8,128)(2,1)S(1)} %copy.27.qt_ref, s32[8,1,512]{2,1,0:T(1,128)S(1)} %copy-done.1, f32[2,512]{1,0:T(2,128)S(1)} %copy-done.5, bf16[1024,128]{1,0:T(8,128)(2,1)S(1)} %get-tuple-element.22.refs_0_, ...), custom_call_target="tpu_custom_call", output_to_operand_aliasing={{0}: (5, {}), {1}: (6, {})} | custom-call | flops 1000 | tf_op jit(solution)/shard_map/attend_earlier/pallas_call | solution.py:186
  52.7 0.0 collective-permute-done.3.refs_0_
  52.8 0.6 attend_earlier.5
  53.3 34.7 %all_to_all.5 = bf16[8,64,1024]{2,1,0:T(8,128)(2,1)S(1)} all-to-all(bf16[8,64,1024]{2,1,0:T(8,128)(2,1)S(1)} %attend_earlier.5), channel_id=1, replica_groups=mesh['ctx'=64,'kvh'=8] {'kvh'}, dimensions={0} | all-to-all | bytes 2097152 | tf_op jit(solution)/shard_map/all_to_all | solution.py:256
  88.1 1.1 %copy.29 = bf16[8,8,8,1024]{3,2,0,1:T(8,128)(2,1)} copy(bf16[8,8,8,1024]{3,2,1,0:T(8,128)(2,1)S(1)} %bitcast.10) | data formatting | bytes 2097152 | tf_op jit(solution)/shard_map/reshape | solution.py:257
  (7 shorter events, 0.0 us)
Async XLA Ops:
  1.7 16.9 %collective-permute-start = (bf16[1024,128]{1,0:T(8,128)(2,1)}, bf16[1024,128]{1,0:T(8,128)(2,1)S(1)}, u32[]{:S(2)}, u32[]{:S(2)}) collective-permute-start(bf16[1024,128]{1,0:T(8,128)(2,1)} %pad_maximum_fusion.kv_ref.near_ref), channel_id=1, source_target_pairs={{0,16},{8,24},{16,32},{24,40},{32,48},{40,56},{48,64},{56,72},{64,... | collective-permute-start | bytes 786440 | tf_op jit(solution)/shard_map/ppermute | solution.py:24
  10.9 0.7 copy-start
  15.8 0.6 copy-start.3
  19.6 22.6 %copy-start.5 = (f32[2,512]{1,0:T(2,128)S(1)}, f32[2,512]{1,0:T(2,128)}, u32[]{:S(2)}) copy-start(f32[2,512]{1,0:T(2,128)} %copy-done.3) | copy-start | bytes 12292
  19.6 5.1 %collective-permute-start.2 = (bf16[1024,128]{1,0:T(8,128)(2,1)S(1)}, bf16[1024,128]{1,0:T(8,128)(2,1)S(1)}, u32[]{:S(2)}, u32[]{:S(2)}) collective-permute-start(bf16[1024,128]{1,0:T(8,128)(2,1)S(1)} %get-tuple-element.19), channel_id=1, source_target_pairs={{0,8},{8,0},{16,24},{24,16},{32,40},{40,32},{48,56},{56,48},{64,72... | collective-permute-start | bytes 786440 | tf_op jit(solution)/shard_map/ppermute | solution.py:29
  22.7 13.4 %collective-permute-start.1 = (bf16[1024,128]{1,0:T(8,128)(2,1)S(1)}, bf16[1024,128]{1,0:T(8,128)(2,1)S(1)}, u32[]{:S(2)}, u32[]{:S(2)}) collective-permute-start(bf16[1024,128]{1,0:T(8,128)(2,1)S(1)} %get-tuple-element.18.refs_0_.near_ref), channel_id=1, source_target_pairs={{0,16},{8,24},{16,32},{24,40},{32,48},{40,56},{48,64},{56,72},{64,... | collective-permute-start | bytes 786440 | tf_op jit(solution)/shard_map/ppermute | solution.py:24
  24.7 0.7 copy-start.1
  25.4 0.7 copy-start.4
  36.1 16.6 %copy-start.2 = (s32[8,1,512]{2,1,0:T(1,128)S(1)}, s32[8,1,512]{2,1,0:T(1,128)}, u32[]{:S(2)}) copy-start(s32[8,1,512]{2,1,0:T(1,128)} %tile.12.first_ref) | copy-start | bytes 49156
  36.2 6.0 %collective-permute-start.4 = (bf16[1024,128]{1,0:T(8,128)(2,1)S(1)}, bf16[1024,128]{1,0:T(8,128)(2,1)S(1)}, u32[]{:S(2)}, u32[]{:S(2)}) collective-permute-start(bf16[1024,128]{1,0:T(8,128)(2,1)S(1)} %get-tuple-element.23), channel_id=1, source_target_pairs={{0,8},{8,0},{16,24},{24,16},{32,40},{40,32},{48,56},{56,48},{64,72... | collective-permute-start | bytes 786440 | tf_op jit(solution)/shard_map/ppermute | solution.py:29
  38.2 14.6 %collective-permute-start.3 = (bf16[1024,128]{1,0:T(8,128)(2,1)S(1)}, bf16[1024,128]{1,0:T(8,128)(2,1)S(1)}, u32[]{:S(2)}, u32[]{:S(2)}) collective-permute-start(bf16[1024,128]{1,0:T(8,128)(2,1)S(1)} %get-tuple-element.22.refs_0_), channel_id=1, source_target_pairs={{0,8},{8,16},{16,24},{24,32},{32,40},{40,48},{48,56},{56,64},{64,7... | collective-permute-start | bytes 786440 | tf_op jit(solution)/shard_map/ppermute | solution.py:24

commit v4 on v3

v4 whole, which is shorter than its diff:
```python
import functools
import math

import jax
import jax.numpy as jnp
from jax import lax
from jax.experimental import pallas as pl
from jax.experimental.pallas import tpu as pltpu
from jax.sharding import PartitionSpec as P

SPAN = 5
DOCS = 32
EXTRA = 8
ROOM = 100.0
VMEM = pl.BlockSpec(memory_space=pltpu.VMEM)
ANY = pl.BlockSpec(memory_space=pl.ANY)
PARAMS = pltpu.CompilerParams(vmem_limit_bytes=16 * 2**20)
COST = pl.CostEstimate(flops=1000, bytes_accessed=0, transcendentals=0)
bf16, f32, i32 = jnp.bfloat16, jnp.float32, jnp.int32


def hop(value, steps):
    count = lax.axis_size("ctx")
    return lax.ppermute(value, "ctx", [(i, i + steps) for i in range(count - steps)])


def scores_of(keys, qt):
    scale = math.log2(math.e) / math.sqrt(keys.shape[1])
    return jnp.dot(keys, qt, preferred_element_type=f32) * scale


def one_row(width):
    return (lax.broadcasted_iota(i32, (EXTRA, width), 0) == 0).astype(bf16)


def own_kernel(qt_ref, near_ref, kv_ref, state_ref, done_ref, vt_ref, *, part):
    chunks, dim, rows = qt_ref.shape
    tok = kv_ref.shape[0] // 2
    lanes = near_ref.shape[1]
    vt_ref[:dim, :] = kv_ref[tok:, :].T
    vt_ref[dim:, :] = one_row(tok)

    near = near_ref[...]
    mine = near[SPAN * tok // lanes :]
    begins = jnp.zeros(mine.shape, i32)
    for doc in range(DOCS):
        before = jnp.sum((near < doc).astype(f32), axis=(0, 1), keepdims=True)
        begins = jnp.where(mine == doc, before.astype(i32), begins)

    place = lax.broadcasted_iota(i32, (1, rows), 1) & (part - 1)
    for chunk in range(chunks):
        at, lane = divmod(chunk * part, lanes)
        first = jnp.concatenate([begins[at : at + 1, lane : lane + part]] * (rows // part), 1)
        width = min(tok, (chunk * part + part + 127) // 128 * 128)
        scores = scores_of(kv_ref[:width, :], qt_ref[chunk])
        own = chunk * part + place
        key = lax.broadcasted_iota(i32, (width, rows), 0)
        scores = jnp.where((key >= first - SPAN * tok) & (key <= own), scores, -1e30)
        row_max = jnp.max(scores, axis=0, keepdims=True)
        raised = jnp.exp2(scores - row_max).astype(bf16)
        state_ref[chunk] = jnp.dot(vt_ref[:, :width], raised, preferred_element_type=f32)
        state_ref[chunk, dim + 1 : dim + 2] = row_max
        state_ref[chunk, dim + 2 : dim + 3] = first.astype(f32)
        squares = jnp.square(qt_ref[chunk].astype(f32))
        state_ref[chunk, dim + 3 : dim + 4] = jnp.sum(squares, axis=0, keepdims=True)
    done_ref[...] = jnp.zeros_like(done_ref)


def earlier_kernel(qt_ref, *refs, base, part, last):
    if last:
        *blocks, state_ref, out_ref, keys_ref, vt_ref = refs
    else:
        *blocks, state_ref, out_ref, done_ref, keys_ref, vt_ref = refs
        done_ref[...] = jnp.zeros_like(done_ref)
    chunks, dim, rows = qt_ref.shape
    tok = blocks[0].shape[0] // 2
    width = len(blocks) * tok
    end = float(base + width)

    def leave(chunk, total):
        if last:
            result = (total[:dim] / total[dim : dim + 1]).T.astype(bf16)
            for head in range(rows // part):
                out_ref[chunk, :, head * dim : (head + 1) * dim] = result[
                    head * part : (head + 1) * part
                ]
        else:
            out_ref[chunk] = total

    def keeping(chunk):
        scores = scores_of(keys_ref[...], qt_ref[chunk])
        raised = jnp.exp2(scores - state_ref[chunk, dim + 1 : dim + 2]).astype(bf16)
        added = jnp.dot(vt_ref[...], raised, preferred_element_type=f32)
        inside = state_ref[chunk, dim + 2 : dim + 3] < end
        leave(chunk, state_ref[chunk] + jnp.where(inside, added, 0.0))

    def raising(chunk):
        scores = scores_of(keys_ref[...], qt_ref[chunk])
        key = base + lax.broadcasted_iota(i32, (width, rows), 0)
        first = state_ref[chunk, dim + 2 : dim + 3].astype(i32)
        scores = jnp.where(key >= first, scores, -1e30)
        old = state_ref[chunk, dim + 1 : dim + 2]
        new = jnp.maximum(old, jnp.max(scores, axis=0, keepdims=True))
        raised = jnp.exp2(scores - new).astype(bf16)
        added = jnp.dot(vt_ref[...], raised, preferred_element_type=f32)
        row = lax.broadcasted_iota(i32, (dim + EXTRA, rows), 0)
        factor = jnp.where(row <= dim, jnp.exp2(old - new), 1.0)
        total = state_ref[chunk] * factor + added
        leave(chunk, jnp.where(row == dim + 1, new, total))

    lowest = jnp.min(state_ref[0, dim + 2 : dim + 3])
    needed = lowest < end

    @pl.when(jnp.logical_not(needed))
    def _():
        for chunk in range(chunks):
            leave(chunk, state_ref[chunk])

    @pl.when(needed)
    def _():
        for i, block in enumerate(blocks):
            keys_ref[i * tok : (i + 1) * tok, :] = block[:tok, :]
            vt_ref[:dim, i * tok : (i + 1) * tok] = block[tok:, :].T
        vt_ref[dim:, :] = one_row(width)
        key = base + lax.broadcasted_iota(i32, (1, width), 1)
        vt_ref[...] = jnp.where(key >= lowest.astype(i32), vt_ref[...], 0.0).astype(bf16)

        squares = jnp.square(keys_ref[...].astype(f32))
        bound = jnp.max(jnp.sum(squares, axis=1, keepdims=True))
        bound = bound * (math.log2(math.e) ** 2 / dim * 1.01)
        fits = jnp.ones((1, rows), f32)
        for chunk in range(chunks):
            room = state_ref[chunk, dim + 1 : dim + 2] + ROOM
            fit = (room > 0) & (state_ref[chunk, dim + 3 : dim + 4] * bound <= room * room)
            fits = jnp.where(fit, fits, 0.0)
        small = jnp.min(fits) > 0
        plain = small & (jnp.min(state_ref[chunks - 1, dim + 2 : dim + 3]) < end)

        @pl.when(plain)
        def _():
            for chunk in range(chunks):
                keeping(chunk)

        @pl.when(jnp.logical_not(plain))
        def _():
            def body(chunk, carry):
                some = jnp.min(state_ref[chunk, dim + 2 : dim + 3]) < end

                @pl.when(jnp.logical_not(some))
                def _():
                    leave(chunk, state_ref[chunk])

                @pl.when(some & small)
                def _():
                    keeping(chunk)

                @pl.when(some & jnp.logical_not(small))
                def _():
                    raising(chunk)

                return carry

            lax.fori_loop(0, chunks, body, 0)


def attend_own(qt, near, kv, part):
    chunks, dim, rows = qt.shape
    tok = kv.shape[0] // 2
    return pl.pallas_call(
        functools.partial(own_kernel, part=part),
        in_specs=[VMEM] * 3,
        out_specs=[VMEM] * 2,
        out_shape=[
            jax.ShapeDtypeStruct((chunks, dim + EXTRA, rows), f32),
            jax.ShapeDtypeStruct((8, 128), f32),
        ],
        scratch_shapes=[pltpu.VMEM((dim + EXTRA, tok), bf16)],
        compiler_params=PARAMS,
        cost_estimate=COST,
        name="attend_own",
    )(qt, near, kv)


def attend_earlier(qt, blocks, base, state, part, last=False):
    chunks, dim, rows = qt.shape
    width = len(blocks) * blocks[0].shape[0] // 2
    if last:
        out_shape = jax.ShapeDtypeStruct((chunks, part, rows // part * dim), bf16)
        out_specs, alias = VMEM, {}
    else:
        out_shape = [
            jax.ShapeDtypeStruct(state.shape, f32),
            jax.ShapeDtypeStruct((8, 128), f32),
        ]
        out_specs = [VMEM] * 2
        alias = {1 + len(blocks): 0}
    return pl.pallas_call(
        functools.partial(earlier_kernel, base=base, part=part, last=last),
        in_specs=[VMEM] * (2 + len(blocks)),
        out_specs=out_specs,
        out_shape=out_shape,
        input_output_aliases=alias,
        scratch_shapes=[
            pltpu.VMEM((width, dim), bf16),
            pltpu.VMEM((dim + EXTRA, width), bf16),
        ],
        compiler_params=PARAMS,
        cost_estimate=COST,
        name="attend_earlier",
    )(qt, *blocks, state)


def held_kernel(value_ref, after_ref, out_ref):
    out_ref[...] = value_ref[...]


def held(value, after):
    return pl.pallas_call(
        held_kernel,
        in_specs=[VMEM, ANY],
        out_specs=VMEM,
        out_shape=jax.ShapeDtypeStruct(value.shape, value.dtype),
        compiler_params=PARAMS,
        cost_estimate=COST,
        name="held",
    )(value, after)


def on_device(queries, keys, values, doc_ids):
    tok, heads, dim = queries.shape
    ring = lax.axis_size("kvh")
    part = tok // ring
    own_index = lax.axis_index("ctx")

    width = (SPAN + 1) * tok
    padded = jnp.concatenate([jnp.full((SPAN * tok,), -1, i32), doc_ids])
    near = lax.dynamic_slice_in_dim(padded, own_index * tok, width, 0).reshape(-1, 128)

    qt = queries.reshape(ring, part, heads, dim).transpose(0, 3, 2, 1)
    qt = qt.reshape(ring, dim, heads * part)

    kv0 = jnp.concatenate([keys[:, 0], values[:, 0]], 0)
    kv2 = hop(kv0, 2)
    kv1 = hop(held(kv0, qt), 1)
    state, done = attend_own(qt, near, kv0, part)
    kv4 = hop(held(kv2, done), 2)
    state, done = attend_earlier(qt, [kv2, kv1], 3 * tok, state, part)
    kv3 = hop(held(kv2, done), 1)
    kv5 = hop(held(kv4, done), 1)
    state, done = attend_earlier(qt, [kv4, kv3], tok, state, part)
    pieces = attend_earlier(qt, [kv5], 0, state, part, last=True)
    pieces = lax.all_to_all(pieces, "kvh", split_axis=0, concat_axis=0, tiled=True)
    return pieces.transpose(1, 0, 2).reshape(part, ring * heads * dim)


def solution(mesh):
    in_specs = (P("ctx", "kvh", None), P("ctx", "kvh", None), P("ctx", "kvh", None), P())
    out_specs = P(("ctx", "kvh"), None)
    return jax.shard_map(
        on_device, mesh=mesh, in_specs=in_specs, out_specs=out_specs, check_vma=False
    )
```

time: 89.8 us -> 74.1 us (0.83)
  the two profiles are of different devices: /device:TPU:3 before, /device:TPU:6 now
where the time goes in v4:
time: 74.1 us; the launch traced here: 73.5 us
  blocking collectives  31 us (42%)
  Pallas kernels  13.5 us (18%)
  waiting for transfers between devices  12.7 us (17%)
  starting transfers between devices  12 us (16%)
  local copies, waits for them, and re-layouts  3.18 us (4%)
  other arithmetic  0.99 us (1%)
    all_to_all x1, blocking collectives, on_device(): lax.all_to_all(pieces, 'kvh', split_axis=0, concat_axis=0, tiled=True)  31 us
    ppermute x5, waiting for transfers between devices, hop(): lax.ppermute(value, 'ctx', [(i, i + steps) for i in range(count - steps)])  12.7 us
    ppermute x5, starting transfers between devices, hop(): lax.ppermute(value, 'ctx', [(i, i + steps) for i in range(count - steps)])  12 us
    pallas_call x3, Pallas kernels, attend_earlier(): pl.pallas_call(functools.partial(earlier_kernel, base=base, part=part, la...  10.3 us
    pallas_call x1, Pallas kernels, attend_own(): pl.pallas_call(functools.partial(own_kernel, part=part), in_specs=[VMEM]...  3.15 us
    transpose x1, local copies, waits for them, and re-layouts, on_device(): qt = queries.reshape(ring, part, heads, dim).transpose(0, 3, 2, 1)  1.5 us
  transfers between devices with their start and end apart: 5, of which 3 were waited for; matrix products, arithmetic and copies ran while one was open for 3% of the time, Pallas kernels for 18%

profile of v4, /device:TPU:6, one launch (start us, length us, event | category | flops | bytes accessed | tf_op | source)
XLA Modules:
  0.0 73.5 jit_solution(10859069992798872799)
XLA Ops:
  0.0 1.0 %pad_maximum_fusion.kv_ref.value_ref = bf16[1024,128]{1,0:T(8,128)(2,1)S(1)} fusion(bf16[512,128]{1,0:T(8,128)(2,1)} %bitcast.14, bf16[512,128]{1,0:T(8,128)(2,1)} %bitcast.15), kind=kLoop, calls=%fused_computation | loop fusion | flops 524288 | bytes 524288 | tf_op jit(solution)/shard_map/concatenate | solution.py:242
  1.0 4.3 %collective-permute-start = (bf16[1024,128]{1,0:T(8,128)(2,1)S(1)}, bf16[1024,128]{1,0:T(8,128)(2,1)S(1)}, u32[]{:S(2)}, u32[]{:S(2)}) collective-permute-start(bf16[1024,128]{1,0:T(8,128)(2,1)S(1)} %pad_maximum_fusion.kv_ref.value_ref), channel_id=1, source_target_pairs={{0,16},{8,24},{16,32},{24,40},{32,48},{40,56},{48,64},{56,72},{64,... | collective-permute-start | bytes 786440 | tf_op jit(solution)/shard_map/ppermute | solution.py:24
  5.3 1.5 %copy.14 = bf16[8,128,8,64]{1,3,2,0:T(8,128)(2,1)S(1)} copy(bf16[8,128,8,64]{1,2,3,0:T(8,128)(2,1)} %bitcast.13) | data formatting | bytes 2097152 | tf_op jit(solution)/shard_map/transpose | solution.py:239
  6.8 0.0 copy-start
  6.8 0.5 copy.19.qt_ref.after_ref
  7.4 1.9 %collective-permute-start.2 = (bf16[1024,128]{1,0:T(8,128)(2,1)S(1)}, bf16[1024,128]{1,0:T(8,128)(2,1)S(1)}, u32[]{:S(2)}, u32[]{:S(2)}) collective-permute-start(bf16[1024,128]{1,0:T(8,128)(2,1)S(1)} %held.5), channel_id=1, source_target_pairs={{0,8},{8,16},{16,24},{24,32},{32,40},{40,48},{48,56},{56,64},{64,7... | collective-permute-start | bytes 786440 | tf_op jit(solution)/shard_map/ppermute | solution.py:24
  9.3 0.0 copy-done
  9.3 0.1 fusion.near_ref
  9.4 3.1 %attend_own.1 = (f32[8,136,512]{2,1,0:T(8,128)S(1)}, f32[8,128]{1,0:T(8,128)S(1)}) custom-call(bf16[8,128,512]{2,1,0:T(8,128)(2,1)S(1)} %copy.19.qt_ref.after_ref, s32[24,128]{1,0:T(8,128)S(1)} %fusion.near_ref, bf16[1024,128]{1,0:T(8,128)(2,1)S(1)} %pad_maximum_fusion.kv_ref.value_ref), custom_call_target="tpu_custom_call" | custom-call | flops 1000 | tf_op jit(solution)/shard_map/attend_own/pallas_call | solution.py:169
  12.5 6.8 %collective-permute-done.value_ref.refs_0_ = bf16[1024,128]{1,0:T(8,128)(2,1)S(1)} collective-permute-done((bf16[1024,128]{1,0:T(8,128)(2,1)S(1)}, bf16[1024,128]{1,0:T(8,128)(2,1)S(1)}, u32[]{:S(2)}, u32[]{:S(2)}) %collective-permute-start) | collective-permute-done | bytes 262176 | tf_op jit(solution)/shard_map/ppermute | solution.py:24
  19.4 1.9 %collective-permute-start.1 = (bf16[1024,128]{1,0:T(8,128)(2,1)S(1)}, bf16[1024,128]{1,0:T(8,128)(2,1)S(1)}, u32[]{:S(2)}, u32[]{:S(2)}) collective-permute-start(bf16[1024,128]{1,0:T(8,128)(2,1)S(1)} %held.4), channel_id=1, source_target_pairs={{0,16},{8,24},{16,32},{24,40},{32,48},{40,56},{48,64},{56,72},{64,... | collective-permute-start | bytes 786440 | tf_op jit(solution)/shard_map/ppermute | solution.py:24
  21.3 0.0 collective-permute-done.2.refs_1_
  21.3 4.4 %attend_earlier.3 = (f32[8,136,512]{2,1,0:T(8,128)S(1)}, f32[8,128]{1,0:T(8,128)S(1)}) custom-call(bf16[8,128,512]{2,1,0:T(8,128)(2,1)S(1)} %copy.19.qt_ref.after_ref, bf16[1024,128]{1,0:T(8,128)(2,1)S(1)} %collective-permute-done.value_ref.refs_0_, bf16[1024,128]{1,0:T(8,128)(2,1)S(1)} %collective-permute-done.2.refs_1_, ...), custom_call_target="tpu_custom_call", output_to_operand_aliasing={{0}: (3, {})} | custom-call | flops 1000 | tf_op jit(solution)/shard_map/attend_earlier/pallas_call | solution.py:197
  25.8 1.9 %collective-permute-start.4 = (bf16[1024,128]{1,0:T(8,128)(2,1)S(1)}, bf16[1024,128]{1,0:T(8,128)(2,1)S(1)}, u32[]{:S(2)}, u32[]{:S(2)}) collective-permute-start(bf16[1024,128]{1,0:T(8,128)(2,1)S(1)} %held.7), channel_id=1, source_target_pairs={{0,8},{8,16},{16,24},{24,32},{32,40},{40,48},{48,56},{56,64},{64,7... | collective-permute-start | bytes 786440 | tf_op jit(solution)/shard_map/ppermute | solution.py:24
  27.7 2.3 %collective-permute-done.1.value_ref.refs_0_ = bf16[1024,128]{1,0:T(8,128)(2,1)S(1)} collective-permute-done((bf16[1024,128]{1,0:T(8,128)(2,1)S(1)}, bf16[1024,128]{1,0:T(8,128)(2,1)S(1)}, u32[]{:S(2)}, u32[]{:S(2)}) %collective-permute-start.1) | collective-permute-done | bytes 262176 | tf_op jit(solution)/shard_map/ppermute | solution.py:24
  30.0 1.9 %collective-permute-start.3 = (bf16[1024,128]{1,0:T(8,128)(2,1)S(1)}, bf16[1024,128]{1,0:T(8,128)(2,1)S(1)}, u32[]{:S(2)}, u32[]{:S(2)}) collective-permute-start(bf16[1024,128]{1,0:T(8,128)(2,1)S(1)} %held.6), channel_id=1, source_target_pairs={{0,8},{8,16},{16,24},{24,32},{32,40},{40,48},{48,56},{56,64},{64,7... | collective-permute-start | bytes 786440 | tf_op jit(solution)/shard_map/ppermute | solution.py:24
  32.0 3.6 %collective-permute-done.4.refs_1_ = bf16[1024,128]{1,0:T(8,128)(2,1)S(1)} collective-permute-done((bf16[1024,128]{1,0:T(8,128)(2,1)S(1)}, bf16[1024,128]{1,0:T(8,128)(2,1)S(1)}, u32[]{:S(2)}, u32[]{:S(2)}) %collective-permute-start.4) | collective-permute-done | bytes 262176 | tf_op jit(solution)/shard_map/ppermute | solution.py:24
  35.6 5.4 %attend_earlier.4 = (f32[8,136,512]{2,1,0:T(8,128)S(1)}, f32[8,128]{1,0:T(8,128)}) custom-call(bf16[8,128,512]{2,1,0:T(8,128)(2,1)S(1)} %copy.19.qt_ref.after_ref, bf16[1024,128]{1,0:T(8,128)(2,1)S(1)} %collective-permute-done.1.value_ref.refs_0_, bf16[1024,128]{1,0:T(8,128)(2,1)S(1)} %collective-permute-done.4.refs_1_, ...), custom_call_target="tpu_custom_call", output_to_operand_aliasing={{0}: (3, {})} | custom-call | flops 1000 | tf_op jit(solution)/shard_map/attend_earlier/pallas_call | solution.py:197
  41.0 0.0 collective-permute-done.3.refs_0_
  41.0 0.5 attend_earlier.5
  41.5 31.0 %all_to_all.5 = bf16[8,64,1024]{2,1,0:T(8,128)(2,1)S(1)} all-to-all(bf16[8,64,1024]{2,1,0:T(8,128)(2,1)S(1)} %attend_earlier.5), channel_id=1, replica_groups=mesh['ctx'=64,'kvh'=8] {'kvh'}, dimensions={0} | all-to-all | bytes 2097152 | tf_op jit(solution)/shard_map/all_to_all | solution.py:252
  72.5 1.1 %copy.21 = bf16[8,8,8,1024]{3,2,0,1:T(8,128)(2,1)} copy(bf16[8,8,8,1024]{3,2,1,0:T(8,128)(2,1)S(1)} %bitcast.11) | data formatting | bytes 2097152 | tf_op jit(solution)/shard_map/reshape | solution.py:253
  (4 shorter events, 0.1 us)
Async XLA Ops:
  1.0 18.3 %collective-permute-start = (bf16[1024,128]{1,0:T(8,128)(2,1)S(1)}, bf16[1024,128]{1,0:T(8,128)(2,1)S(1)}, u32[]{:S(2)}, u32[]{:S(2)}) collective-permute-start(bf16[1024,128]{1,0:T(8,128)(2,1)S(1)} %pad_maximum_fusion.kv_ref.value_ref), channel_id=1, source_target_pairs={{0,16},{8,24},{16,32},{24,40},{32,48},{40,56},{48,64},{56,72},{64,... | collective-permute-start | bytes 786440 | tf_op jit(solution)/shard_map/ppermute | solution.py:24
  6.8 2.5 %copy-start = (s32[32768]{0:T(1024)S(1)}, s32[32768]{0:T(1024)}, u32[]{:S(2)}) copy-start(s32[32768]{0:T(1024)} %param.7) | copy-start | bytes 393220
  7.4 13.9 %collective-permute-start.2 = (bf16[1024,128]{1,0:T(8,128)(2,1)S(1)}, bf16[1024,128]{1,0:T(8,128)(2,1)S(1)}, u32[]{:S(2)}, u32[]{:S(2)}) collective-permute-start(bf16[1024,128]{1,0:T(8,128)(2,1)S(1)} %held.5), channel_id=1, source_target_pairs={{0,8},{8,16},{16,24},{24,32},{32,40},{40,48},{48,56},{56,64},{64,7... | collective-permute-start | bytes 786440 | tf_op jit(solution)/shard_map/ppermute | solution.py:24
  19.4 10.7 %collective-permute-start.1 = (bf16[1024,128]{1,0:T(8,128)(2,1)S(1)}, bf16[1024,128]{1,0:T(8,128)(2,1)S(1)}, u32[]{:S(2)}, u32[]{:S(2)}) collective-permute-start(bf16[1024,128]{1,0:T(8,128)(2,1)S(1)} %held.4), channel_id=1, source_target_pairs={{0,16},{8,24},{16,32},{24,40},{32,48},{40,56},{48,64},{56,72},{64,... | collective-permute-start | bytes 786440 | tf_op jit(solution)/shard_map/ppermute | solution.py:24
  25.8 9.8 %collective-permute-start.4 = (bf16[1024,128]{1,0:T(8,128)(2,1)S(1)}, bf16[1024,128]{1,0:T(8,128)(2,1)S(1)}, u32[]{:S(2)}, u32[]{:S(2)}) collective-permute-start(bf16[1024,128]{1,0:T(8,128)(2,1)S(1)} %held.7), channel_id=1, source_target_pairs={{0,8},{8,16},{16,24},{24,32},{32,40},{40,48},{48,56},{56,64},{64,7... | collective-permute-start | bytes 786440 | tf_op jit(solution)/shard_map/ppermute | solution.py:24
  30.0 10.9 %collective-permute-start.3 = (bf16[1024,128]{1,0:T(8,128)(2,1)S(1)}, bf16[1024,128]{1,0:T(8,128)(2,1)S(1)}, u32[]{:S(2)}, u32[]{:S(2)}) collective-permute-start(bf16[1024,128]{1,0:T(8,128)(2,1)S(1)} %held.6), channel_id=1, source_target_pairs={{0,8},{8,16},{16,24},{24,32},{32,40},{40,48},{48,56},{56,64},{64,7... | collective-permute-start | bytes 786440 | tf_op jit(solution)/shard_map/ppermute | solution.py:24

commit v5 on v4

--- a/solution.py
+++ b/solution.py
@@ -19,9 +19,15 @@
 bf16, f32, i32 = jnp.bfloat16, jnp.float32, jnp.int32
 
 
-def hop(value, steps):
+def hop(value, steps, begin=0, stride=1):
     count = lax.axis_size("ctx")
-    return lax.ppermute(value, "ctx", [(i, i + steps) for i in range(count - steps)])
+    pairs = [(i, i + steps) for i in range(begin, count - steps, stride)]
+    return lax.ppermute(value, "ctx", pairs)
+
+
+def swap_cores(value):
+    count = lax.axis_size("ctx")
+    return lax.ppermute(value, "ctx", [(i, i ^ 1) for i in range(count)])
 
 
 def scores_of(keys, qt):
@@ -68,9 +74,9 @@
 
 def earlier_kernel(qt_ref, *refs, base, part, last):
     if last:
-        *blocks, state_ref, out_ref, keys_ref, vt_ref = refs
+        *blocks, state_ref, _, out_ref, keys_ref, vt_ref = refs
     else:
-        *blocks, state_ref, out_ref, done_ref, keys_ref, vt_ref = refs
+        *blocks, state_ref, _, out_ref, done_ref, keys_ref, vt_ref = refs
         done_ref[...] = jnp.zeros_like(done_ref)
     chunks, dim, rows = qt_ref.shape
     tok = blocks[0].shape[0] // 2
@@ -181,7 +187,7 @@
     )(qt, near, kv)
 
 
-def attend_earlier(qt, blocks, base, state, part, last=False):
+def attend_earlier(qt, blocks, base, state, part, after, last=False):
     chunks, dim, rows = qt.shape
     width = len(blocks) * blocks[0].shape[0] // 2
     if last:
@@ -196,7 +202,7 @@
         alias = {1 + len(blocks): 0}
     return pl.pallas_call(
         functools.partial(earlier_kernel, base=base, part=part, last=last),
-        in_specs=[VMEM] * (2 + len(blocks)),
+        in_specs=[VMEM] * (2 + len(blocks)) + [ANY],
         out_specs=out_specs,
         out_shape=out_shape,
         input_output_aliases=alias,
@@ -207,23 +213,67 @@
         compiler_params=PARAMS,
         cost_estimate=COST,
         name="attend_earlier",
-    )(qt, *blocks, state)
+    )(qt, *blocks, state, after)
 
 
 def held_kernel(value_ref, after_ref, out_ref):
     out_ref[...] = value_ref[...]
 
 
-def held(value, after):
+def arrived_kernel(value_ref, out_ref):
+    out_ref[...] = jnp.zeros_like(out_ref)
+
+
+def sum_kernel(one_ref, other_ref, after_ref, out_ref):
+    out_ref[...] = one_ref[...] + other_ref[...]
+
+
+def chosen_kernel(one_ref, other_ref, after_ref, out_ref):
+    odd = lax.rem(lax.axis_index("ctx"), 2) == 1
+
+    @pl.when(odd)
+    def _():
+        out_ref[...] = other_ref[...]
+
+    @pl.when(jnp.logical_not(odd))
+    def _():
+        out_ref[...] = one_ref[...]
+
+
+def small_call(kernel, name, values, after):
     return pl.pallas_call(
-        held_kernel,
-        in_specs=[VMEM, ANY],
+        kernel,
+        in_specs=[VMEM] * len(values) + [ANY],
         out_specs=VMEM,
-        out_shape=jax.ShapeDtypeStruct(value.shape, value.dtype),
+        out_shape=jax.ShapeDtypeStruct(values[0].shape, values[0].dtype),
         compiler_params=PARAMS,
         cost_estimate=COST,
-        name="held",
-    )(value, after)
+        name=name,
+    )(*values, after)
+
+
+def held(value, after):
+    return small_call(held_kernel, "held", [value], after)
+
+
+def arrived(value):
+    return pl.pallas_call(
+        arrived_kernel,
+        in_specs=[ANY],
+        out_specs=VMEM,
+        out_shape=jax.ShapeDtypeStruct((8, 128), f32),
+        compiler_params=PARAMS,
+        cost_estimate=COST,
+        name="arrived",
+    )(value)
+
+
+def joined(one, other, after):
+    return small_call(sum_kernel, "joined", [one, other], after)
+
+
+def chosen(even, odd, after):
+    return small_call(chosen_kernel, "chosen", [even, odd], after)
 
 
 def on_device(queries, keys, values, doc_ids):
@@ -240,15 +290,20 @@
     qt = qt.reshape(ring, dim, heads * part)
 
     kv0 = jnp.concatenate([keys[:, 0], values[:, 0]], 0)
-    kv2 = hop(kv0, 2)
-    kv1 = hop(held(kv0, qt), 1)
+    odd2 = hop(kv0, 2, 1, 2)
+    even2 = hop(held(kv0, qt), 2, 0, 2)
     state, done = attend_own(qt, near, kv0, part)
-    kv4 = hop(held(kv2, done), 2)
-    state, done = attend_earlier(qt, [kv2, kv1], 3 * tok, state, part)
-    kv3 = hop(held(kv2, done), 1)
-    kv5 = hop(held(kv4, done), 1)
-    state, done = attend_earlier(qt, [kv4, kv3], tok, state, part)
-    pieces = attend_earlier(qt, [kv5], 0, state, part, last=True)
+    sent = held(odd2, done)
+    odd4 = hop(sent, 2, 1, 2)
+    kv1 = swap_cores(chosen(kv0, odd2, sent))
+    kv2 = joined(odd2, even2, done)
+    even4 = hop(held(even2, done), 2, 0, 2)
+    state, done = attend_earlier(qt, [kv2, kv1], 3 * tok, state, part, arrived(odd4))
+    kv3 = swap_cores(chosen(even2, odd4, done))
+    kv4 = joined(odd4, even4, done)
+    kv5 = hop(kv4, 1)
+    state, done = attend_earlier(qt, [kv4, kv3], tok, state, part, done)
+    pieces = attend_earlier(qt, [kv5], 0, state, part, done, last=True)
     pieces = lax.all_to_all(pieces, "kvh", split_axis=0, concat_axis=0, tiled=True)
     return pieces.transpose(1, 0, 2).reshape(part, ring * heads * dim)
 

time: 74.1 us -> 78.2 us (1.055)
  starting transfers between devices: 12 us -> 22 us
  waiting for transfers between devices: 12.7 us -> 3.02 us
  blocking collectives: 31 us -> 34.4 us
    ppermute x5 -> x7, starting transfers between devices: 12 us -> 22 us  [the longest x2 12.5 us: swap_cores(): return lax.ppermute(value, 'ctx', [(i, i ^ 1) for i in range(count)])]
    ppermute x5 -> x7, waiting for transfers between devices: 12.7 us -> 3.02 us  [the longest x5 3.02 us: hop(): return lax.ppermute(value, 'ctx', pairs)]
    all_to_all x1, blocking collectives: 31 us -> 34.4 us  [on_device(): lax.all_to_all(pieces, 'kvh', split_axis=0, concat_axis=0, tiled=True)]
  transfers between devices with their start and end apart: 5 -> 7, of which waited for: 3 -> 1; matrix products, arithmetic and copies ran while one was open for 3% -> 3% of each run, Pallas kernels for 18% -> 16%
where the time goes in v5:
time: 78.2 us; the launch traced here: 77 us
  blocking collectives  34.4 us (44%)
  starting transfers between devices  22 us (28%)
  Pallas kernels  13.2 us (17%)
  local copies, waits for them, and re-layouts  3.18 us (4%)
  waiting for transfers between devices  3.02 us (4%)
  other arithmetic  0.99 us (1%)
    all_to_all x1, blocking collectives, on_device(): lax.all_to_all(pieces, 'kvh', split_axis=0, concat_axis=0, tiled=True)  34.4 us
    ppermute x2, starting transfers between devices, swap_cores(): return lax.ppermute(value, 'ctx', [(i, i ^ 1) for i in range(count)])  12.5 us
    pallas_call x3, Pallas kernels, attend_earlier(): pl.pallas_call(functools.partial(earlier_kernel, base=base, part=part, la...  9.78 us
    ppermute x5, starting transfers between devices, hop(): return lax.ppermute(value, 'ctx', pairs)  9.48 us
    pallas_call x1, Pallas kernels, attend_own(): pl.pallas_call(functools.partial(own_kernel, part=part), in_specs=[VMEM]...  3.15 us
    ppermute x5, waiting for transfers between devices, hop(): return lax.ppermute(value, 'ctx', pairs)  3.02 us
  transfers between devices with their start and end apart: 7, of which 1 were waited for; matrix products, arithmetic and copies ran while one was open for 3% of the time, Pallas kernels for 16%

profile of v5, /device:TPU:6, one launch (start us, length us, event | category | flops | bytes accessed | tf_op | source)
XLA Modules:
  0.0 77.0 jit_solution(12820101403589030822)
XLA Ops:
  0.0 1.0 %pad_maximum_fusion.kv_ref.value_ref.one_ref = bf16[1024,128]{1,0:T(8,128)(2,1)S(1)} fusion(bf16[512,128]{1,0:T(8,128)(2,1)} %bitcast.14, bf16[512,128]{1,0:T(8,128)(2,1)} %bitcast.15), kind=kLoop, calls=%fused_computation | loop fusion | flops 524288 | bytes 524288 | tf_op jit(solution)/shard_map/concatenate | solution.py:292
  1.0 0.7 collective-permute-start
  1.7 1.5 %copy.14 = bf16[8,128,8,64]{1,3,2,0:T(8,128)(2,1)S(1)} copy(bf16[8,128,8,64]{1,2,3,0:T(8,128)(2,1)} %bitcast.13) | data formatting | bytes 2097152 | tf_op jit(solution)/shard_map/transpose | solution.py:289
  3.2 0.0 copy-start
  3.2 0.5 copy.19.qt_ref.after_ref
  3.8 4.3 %collective-permute-start.2 = (bf16[1024,128]{1,0:T(8,128)(2,1)S(1)}, bf16[1024,128]{1,0:T(8,128)(2,1)S(1)}, u32[]{:S(2)}, u32[]{:S(2)}) collective-permute-start(bf16[1024,128]{1,0:T(8,128)(2,1)S(1)} %held.4), channel_id=1, source_target_pairs={{0,16},{16,32},{32,48},{48,64},{64,80},{80,96},{96,112},{112,128},... | collective-permute-start | bytes 786440 | tf_op jit(solution)/shard_map/ppermute | solution.py:25
  8.1 0.0 copy-done
  8.1 0.1 fusion.near_ref
  8.2 3.2 %attend_own.1 = (f32[8,136,512]{2,1,0:T(8,128)S(1)}, f32[8,128]{1,0:T(8,128)S(1)}) custom-call(bf16[8,128,512]{2,1,0:T(8,128)(2,1)S(1)} %copy.19.qt_ref.after_ref, s32[24,128]{1,0:T(8,128)S(1)} %fusion.near_ref, bf16[1024,128]{1,0:T(8,128)(2,1)S(1)} %pad_maximum_fusion.kv_ref.value_ref.one_ref), custom_call_target="tpu_custom_call" | custom-call | flops 1000 | tf_op jit(solution)/shard_map/attend_own/pallas_call | solution.py:175
  11.3 0.0 collective-permute-done.value_ref.one_ref.other_ref
  11.3 0.7 collective-permute-start.1
  12.1 7.3 %collective-permute-start.4 = (bf16[1024,128]{1,0:T(8,128)(2,1)S(1)}, bf16[1024,128]{1,0:T(8,128)(2,1)S(1)}, u32[]{:S(2)}, u32[]{:S(2)}) collective-permute-start(bf16[1024,128]{1,0:T(8,128)(2,1)S(1)} %chosen.2), channel_id=1, source_target_pairs={{0,8},{8,0},{16,24},{24,16},{32,40},{40,32},{48,56},{56,48},{64,72... | collective-permute-start | bytes 786440 | tf_op jit(solution)/shard_map/ppermute | solution.py:30
  19.4 0.0 collective-permute-done.2.value_ref.other_ref.one_ref
  19.5 1.9 %collective-permute-start.3 = (bf16[1024,128]{1,0:T(8,128)(2,1)S(1)}, bf16[1024,128]{1,0:T(8,128)(2,1)S(1)}, u32[]{:S(2)}, u32[]{:S(2)}) collective-permute-start(bf16[1024,128]{1,0:T(8,128)(2,1)S(1)} %held.5), channel_id=1, source_target_pairs={{0,16},{16,32},{32,48},{48,64},{64,80},{80,96},{96,112},{112,128},... | collective-permute-start | bytes 786440 | tf_op jit(solution)/shard_map/ppermute | solution.py:25
  21.4 0.1 joined.2.refs_0_
  21.5 0.0 collective-permute-done.1.value_ref.one_ref.other_ref
  21.5 0.0 collective-permute-done.4.refs_1_
  21.5 4.4 %attend_earlier.3 = (f32[8,136,512]{2,1,0:T(8,128)S(1)}, f32[8,128]{1,0:T(8,128)S(1)}) custom-call(bf16[8,128,512]{2,1,0:T(8,128)(2,1)S(1)} %copy.19.qt_ref.after_ref, bf16[1024,128]{1,0:T(8,128)(2,1)S(1)} %joined.2.refs_0_, bf16[1024,128]{1,0:T(8,128)(2,1)S(1)} %collective-permute-done.4.refs_1_, ...), custom_call_target="tpu_custom_call", output_to_operand_aliasing={{0}: (3, {})} | custom-call | flops 1000 | tf_op jit(solution)/shard_map/attend_earlier/pallas_call | solution.py:203
  26.0 5.2 %collective-permute-start.6 = (bf16[1024,128]{1,0:T(8,128)(2,1)S(1)}, bf16[1024,128]{1,0:T(8,128)(2,1)S(1)}, u32[]{:S(2)}, u32[]{:S(2)}) collective-permute-start(bf16[1024,128]{1,0:T(8,128)(2,1)S(1)} %chosen.3), channel_id=1, source_target_pairs={{0,8},{8,0},{16,24},{24,16},{32,40},{40,32},{48,56},{56,48},{64,72... | collective-permute-start | bytes 786440 | tf_op jit(solution)/shard_map/ppermute | solution.py:30
  31.2 0.0 collective-permute-done.3.other_ref
  31.2 0.1 joined.3.refs_0_
  31.3 1.9 %collective-permute-start.5 = (bf16[1024,128]{1,0:T(8,128)(2,1)S(1)}, bf16[1024,128]{1,0:T(8,128)(2,1)S(1)}, u32[]{:S(2)}, u32[]{:S(2)}) collective-permute-start(bf16[1024,128]{1,0:T(8,128)(2,1)S(1)} %joined.3.refs_0_), channel_id=1, source_target_pairs={{0,8},{8,16},{16,24},{24,32},{32,40},{40,48},{48,56},{56,64},{64,7... | collective-permute-start | bytes 786440 | tf_op jit(solution)/shard_map/ppermute | solution.py:25
  33.2 0.0 collective-permute-done.6.refs_1_
  33.2 4.8 %attend_earlier.4 = (f32[8,136,512]{2,1,0:T(8,128)S(1)}, f32[8,128]{1,0:T(8,128)S(1)}) custom-call(bf16[8,128,512]{2,1,0:T(8,128)(2,1)S(1)} %copy.19.qt_ref.after_ref, bf16[1024,128]{1,0:T(8,128)(2,1)S(1)} %joined.3.refs_0_, bf16[1024,128]{1,0:T(8,128)(2,1)S(1)} %collective-permute-done.6.refs_1_, ...), custom_call_target="tpu_custom_call", output_to_operand_aliasing={{0}: (3, {})} | custom-call | flops 1000 | tf_op jit(solution)/shard_map/attend_earlier/pallas_call | solution.py:203
  38.0 3.0 %collective-permute-done.5.refs_0_ = bf16[1024,128]{1,0:T(8,128)(2,1)S(1)} collective-permute-done((bf16[1024,128]{1,0:T(8,128)(2,1)S(1)}, bf16[1024,128]{1,0:T(8,128)(2,1)S(1)}, u32[]{:S(2)}, u32[]{:S(2)}) %collective-permute-start.5) | collective-permute-done | bytes 262176 | tf_op jit(solution)/shard_map/ppermute | solution.py:25
  41.1 0.5 attend_earlier.5
  41.5 34.4 %all_to_all.5 = bf16[8,64,1024]{2,1,0:T(8,128)(2,1)S(1)} all-to-all(bf16[8,64,1024]{2,1,0:T(8,128)(2,1)S(1)} %attend_earlier.5), channel_id=1, replica_groups=mesh['ctx'=64,'kvh'=8] {'kvh'}, dimensions={0} | all-to-all | bytes 2097152 | tf_op jit(solution)/shard_map/all_to_all | solution.py:307
  76.0 1.1 %copy.21 = bf16[8,8,8,1024]{3,2,0,1:T(8,128)(2,1)} copy(bf16[8,8,8,1024]{3,2,1,0:T(8,128)(2,1)S(1)} %bitcast.11) | data formatting | bytes 2097152 | tf_op jit(solution)/shard_map/reshape | solution.py:308
  (6 shorter events, 0.1 us)
Async XLA Ops:
  1.0 10.3 %collective-permute-start = (bf16[1024,128]{1,0:T(8,128)(2,1)S(1)}, bf16[1024,128]{1,0:T(8,128)(2,1)S(1)}, u32[]{:S(2)}, u32[]{:S(2)}) collective-permute-start(bf16[1024,128]{1,0:T(8,128)(2,1)S(1)} %pad_maximum_fusion.kv_ref.value_ref.one_ref), channel_id=1, source_target_pairs={{8,24},{24,40},{40,56},{56,72},{72,88},{88,104},{104,120},{120,136... | collective-permute-start | bytes 786440 | tf_op jit(solution)/shard_map/ppermute | solution.py:25
  3.2 4.9 %copy-start = (s32[32768]{0:T(1024)S(1)}, s32[32768]{0:T(1024)}, u32[]{:S(2)}) copy-start(s32[32768]{0:T(1024)} %param.7) | copy-start | bytes 393220
  3.8 15.7 %collective-permute-start.2 = (bf16[1024,128]{1,0:T(8,128)(2,1)S(1)}, bf16[1024,128]{1,0:T(8,128)(2,1)S(1)}, u32[]{:S(2)}, u32[]{:S(2)}) collective-permute-start(bf16[1024,128]{1,0:T(8,128)(2,1)S(1)} %held.4), channel_id=1, source_target_pairs={{0,16},{16,32},{32,48},{48,64},{64,80},{80,96},{96,112},{112,128},... | collective-permute-start | bytes 786440 | tf_op jit(solution)/shard_map/ppermute | solution.py:25
  11.3 10.1 %collective-permute-start.1 = (bf16[1024,128]{1,0:T(8,128)(2,1)S(1)}, bf16[1024,128]{1,0:T(8,128)(2,1)S(1)}, u32[]{:S(2)}, u32[]{:S(2)}) collective-permute-start(bf16[1024,128]{1,0:T(8,128)(2,1)S(1)} %held.3.after_ref), channel_id=1, source_target_pairs={{8,24},{24,40},{40,56},{56,72},{72,88},{88,104},{104,120},{120,136... | collective-permute-start | bytes 786440 | tf_op jit(solution)/shard_map/ppermute | solution.py:25
  12.1 9.4 %collective-permute-start.4 = (bf16[1024,128]{1,0:T(8,128)(2,1)S(1)}, bf16[1024,128]{1,0:T(8,128)(2,1)S(1)}, u32[]{:S(2)}, u32[]{:S(2)}) collective-permute-start(bf16[1024,128]{1,0:T(8,128)(2,1)S(1)} %chosen.2), channel_id=1, source_target_pairs={{0,8},{8,0},{16,24},{24,16},{32,40},{40,32},{48,56},{56,48},{64,72... | collective-permute-start | bytes 786440 | tf_op jit(solution)/shard_map/ppermute | solution.py:30
  19.5 11.7 %collective-permute-start.3 = (bf16[1024,128]{1,0:T(8,128)(2,1)S(1)}, bf16[1024,128]{1,0:T(8,128)(2,1)S(1)}, u32[]{:S(2)}, u32[]{:S(2)}) collective-permute-start(bf16[1024,128]{1,0:T(8,128)(2,1)S(1)} %held.5), channel_id=1, source_target_pairs={{0,16},{16,32},{32,48},{48,64},{64,80},{80,96},{96,112},{112,128},... | collective-permute-start | bytes 786440 | tf_op jit(solution)/shard_map/ppermute | solution.py:25
  26.0 7.2 %collective-permute-start.6 = (bf16[1024,128]{1,0:T(8,128)(2,1)S(1)}, bf16[1024,128]{1,0:T(8,128)(2,1)S(1)}, u32[]{:S(2)}, u32[]{:S(2)}) collective-permute-start(bf16[1024,128]{1,0:T(8,128)(2,1)S(1)} %chosen.3), channel_id=1, source_target_pairs={{0,8},{8,0},{16,24},{24,16},{32,40},{40,32},{48,56},{56,48},{64,72... | collective-permute-start | bytes 786440 | tf_op jit(solution)/shard_map/ppermute | solution.py:30
  31.3 9.8 %collective-permute-start.5 = (bf16[1024,128]{1,0:T(8,128)(2,1)S(1)}, bf16[1024,128]{1,0:T(8,128)(2,1)S(1)}, u32[]{:S(2)}, u32[]{:S(2)}) collective-permute-start(bf16[1024,128]{1,0:T(8,128)(2,1)S(1)} %joined.3.refs_0_), channel_id=1, source_target_pairs={{0,8},{8,16},{16,24},{24,32},{32,40},{40,48},{48,56},{56,64},{64,7... | collective-permute-start | bytes 786440 | tf_op jit(solution)/shard_map/ppermute | solution.py:25

commit v6 on v4

--- a/solution.py
+++ b/solution.py
@@ -11,7 +11,9 @@
 SPAN = 5
 DOCS = 32
 EXTRA = 8
-ROOM = 100.0
+LARGEST_KEY = 5.0
+ROOM = 112.0
+GROUP = 2
 VMEM = pl.BlockSpec(memory_space=pltpu.VMEM)
 ANY = pl.BlockSpec(memory_space=pl.ANY)
 PARAMS = pltpu.CompilerParams(vmem_limit_bytes=16 * 2**20)
@@ -62,7 +64,11 @@
         state_ref[chunk, dim + 1 : dim + 2] = row_max
         state_ref[chunk, dim + 2 : dim + 3] = first.astype(f32)
         squares = jnp.square(qt_ref[chunk].astype(f32))
-        state_ref[chunk, dim + 3 : dim + 4] = jnp.sum(squares, axis=0, keepdims=True)
+        bound = jnp.sum(squares, axis=0, keepdims=True)
+        bound = bound * (math.log2(math.e) ** 2 * LARGEST_KEY**2 * 1.01)
+        room = row_max + ROOM
+        fits = (room > 0) & (bound <= room * room)
+        state_ref[chunk, dim + 3 : dim + 4] = jnp.where(fits, 1.0, 0.0)
     done_ref[...] = jnp.zeros_like(done_ref)
 
 
@@ -87,12 +93,15 @@
         else:
             out_ref[chunk] = total
 
-    def keeping(chunk):
-        scores = scores_of(keys_ref[...], qt_ref[chunk])
-        raised = jnp.exp2(scores - state_ref[chunk, dim + 1 : dim + 2]).astype(bf16)
+    def keeping(*group):
+        qt = jnp.concatenate([qt_ref[c] for c in group], 1)
+        row_max = jnp.concatenate([state_ref[c, dim + 1 : dim + 2] for c in group], 1)
+        raised = jnp.exp2(scores_of(keys_ref[...], qt) - row_max).astype(bf16)
         added = jnp.dot(vt_ref[...], raised, preferred_element_type=f32)
-        inside = state_ref[chunk, dim + 2 : dim + 3] < end
-        leave(chunk, state_ref[chunk] + jnp.where(inside, added, 0.0))
+        for i, chunk in enumerate(group):
+            inside = state_ref[chunk, dim + 2 : dim + 3] < end
+            mine = added[:, i * rows : (i + 1) * rows]
+            leave(chunk, state_ref[chunk] + jnp.where(inside, mine, 0.0))
 
     def raising(chunk):
         scores = scores_of(keys_ref[...], qt_ref[chunk])
@@ -118,49 +127,45 @@
 
     @pl.when(needed)
     def _():
+        fits = state_ref[0, dim + 3 : dim + 4]
+        for chunk in range(1, chunks):
+            fits = jnp.minimum(fits, state_ref[chunk, dim + 3 : dim + 4])
+        small = jnp.min(fits) > 0
         for i, block in enumerate(blocks):
             keys_ref[i * tok : (i + 1) * tok, :] = block[:tok, :]
             vt_ref[:dim, i * tok : (i + 1) * tok] = block[tok:, :].T
         vt_ref[dim:, :] = one_row(width)
-        key = base + lax.broadcasted_iota(i32, (1, width), 1)
-        vt_ref[...] = jnp.where(key >= lowest.astype(i32), vt_ref[...], 0.0).astype(bf16)
-
-        squares = jnp.square(keys_ref[...].astype(f32))
-        bound = jnp.max(jnp.sum(squares, axis=1, keepdims=True))
-        bound = bound * (math.log2(math.e) ** 2 / dim * 1.01)
-        fits = jnp.ones((1, rows), f32)
-        for chunk in range(chunks):
-            room = state_ref[chunk, dim + 1 : dim + 2] + ROOM
-            fit = (room > 0) & (state_ref[chunk, dim + 3 : dim + 4] * bound <= room * room)
-            fits = jnp.where(fit, fits, 0.0)
-        small = jnp.min(fits) > 0
-        plain = small & (jnp.min(state_ref[chunks - 1, dim + 2 : dim + 3]) < end)
+
+        @pl.when(lowest > base)
+        def _():
+            key = base + lax.broadcasted_iota(i32, (1, width), 1)
+            vt_ref[...] = jnp.where(key >= lowest.astype(i32), vt_ref[...], 0.0).astype(bf16)
+
+        groups = [range(c, min(c + GROUP, chunks)) for c in range(0, chunks, GROUP)]
+        plain = small & (jnp.min(state_ref[groups[-1][0], dim + 2 : dim + 3]) < end)
 
         @pl.when(plain)
         def _():
-            for chunk in range(chunks):
-                keeping(chunk)
+            for group in groups:
+                keeping(*group)
 
         @pl.when(jnp.logical_not(plain))
         def _():
-            def body(chunk, carry):
-                some = jnp.min(state_ref[chunk, dim + 2 : dim + 3]) < end
+            for group in groups:
+                some = jnp.min(state_ref[group[0], dim + 2 : dim + 3]) < end
 
                 @pl.when(jnp.logical_not(some))
                 def _():
-                    leave(chunk, state_ref[chunk])
+                    for chunk in group:
+                        leave(chunk, state_ref[chunk])
 
                 @pl.when(some & small)
                 def _():
-                    keeping(chunk)
+                    keeping(*group)
 
                 @pl.when(some & jnp.logical_not(small))
                 def _():
-                    raising(chunk)
-
-                return carry
-
-            lax.fori_loop(0, chunks, body, 0)
+                    lax.fori_loop(group[0], group[-1] + 1, lambda chunk, _: raising(chunk), None)
 
 
 def attend_own(qt, near, kv, part):

time: 74.1 us -> 72 us (0.972)
  waiting for transfers between devices: 12.7 us -> 15.8 us
  Pallas kernels: 13.5 us -> 10.9 us
  blocking collectives: 31 us -> 28.8 us
    ppermute x5, waiting for transfers between devices: 12.7 us -> 15.8 us  [hop(): lax.ppermute(value, 'ctx', [(i, i + steps) for i in range(count - steps)])]
    pallas_call x3, Pallas kernels: 10.3 us -> 7.63 us  [attend_earlier(): pl.pallas_call(functools.partial(earlier_kernel, base=base, part=part, la...]
    all_to_all x1, blocking collectives: 31 us -> 28.8 us  [on_device(): lax.all_to_all(pieces, 'kvh', split_axis=0, concat_axis=0, tiled=True)]
  transfers between devices with their start and end apart: 5 -> 5, of which waited for: 3 -> 4; matrix products, arithmetic and copies ran while one was open for 3% -> 3% of each run, Pallas kernels for 18% -> 12%
where the time goes in v6:
time: 72 us; the launch traced here: 71.7 us
  blocking collectives  28.8 us (40%)
  waiting for transfers between devices  15.8 us (22%)
  starting transfers between devices  12 us (17%)
  Pallas kernels  10.9 us (15%)
  local copies, waits for them, and re-layouts  3.18 us (4%)
  other arithmetic  0.99 us (1%)
    all_to_all x1, blocking collectives, on_device(): lax.all_to_all(pieces, 'kvh', split_axis=0, concat_axis=0, tiled=True)  28.8 us
    ppermute x5, waiting for transfers between devices, hop(): lax.ppermute(value, 'ctx', [(i, i + steps) for i in range(count - steps)])  15.8 us
    ppermute x5, starting transfers between devices, hop(): lax.ppermute(value, 'ctx', [(i, i + steps) for i in range(count - steps)])  12 us
    pallas_call x3, Pallas kernels, attend_earlier(): pl.pallas_call(functools.partial(earlier_kernel, base=base, part=part, la...  7.63 us
    pallas_call x1, Pallas kernels, attend_own(): pl.pallas_call(functools.partial(own_kernel, part=part), in_specs=[VMEM]...  3.15 us
    transpose x1, local copies, waits for them, and re-layouts, on_device(): qt = queries.reshape(ring, part, heads, dim).transpose(0, 3, 2, 1)  1.5 us
  transfers between devices with their start and end apart: 5, of which 4 were waited for; matrix products, arithmetic and copies ran while one was open for 3% of the time, Pallas kernels for 12%

profile of v6, /device:TPU:6, one launch (start us, length us, event | category | flops | bytes accessed | tf_op | source)
XLA Modules:
  0.0 71.7 jit_solution(13277333251254404565)
XLA Ops:
  0.0 1.0 %pad_maximum_fusion.kv_ref.value_ref = bf16[1024,128]{1,0:T(8,128)(2,1)S(1)} fusion(bf16[512,128]{1,0:T(8,128)(2,1)} %bitcast.14, bf16[512,128]{1,0:T(8,128)(2,1)} %bitcast.15), kind=kLoop, calls=%fused_computation | loop fusion | flops 524288 | bytes 524288 | tf_op jit(solution)/shard_map/concatenate | solution.py:247
  1.0 4.3 %collective-permute-start = (bf16[1024,128]{1,0:T(8,128)(2,1)S(1)}, bf16[1024,128]{1,0:T(8,128)(2,1)S(1)}, u32[]{:S(2)}, u32[]{:S(2)}) collective-permute-start(bf16[1024,128]{1,0:T(8,128)(2,1)S(1)} %pad_maximum_fusion.kv_ref.value_ref), channel_id=1, source_target_pairs={{0,16},{8,24},{16,32},{24,40},{32,48},{40,56},{48,64},{56,72},{64,... | collective-permute-start | bytes 786440 | tf_op jit(solution)/shard_map/ppermute | solution.py:26
  5.3 1.5 %copy.14 = bf16[8,128,8,64]{1,3,2,0:T(8,128)(2,1)S(1)} copy(bf16[8,128,8,64]{1,2,3,0:T(8,128)(2,1)} %bitcast.13) | data formatting | bytes 2097152 | tf_op jit(solution)/shard_map/transpose | solution.py:244
  6.8 0.0 copy-start
  6.8 0.5 copy.19.qt_ref.after_ref
  7.4 1.9 %collective-permute-start.2 = (bf16[1024,128]{1,0:T(8,128)(2,1)S(1)}, bf16[1024,128]{1,0:T(8,128)(2,1)S(1)}, u32[]{:S(2)}, u32[]{:S(2)}) collective-permute-start(bf16[1024,128]{1,0:T(8,128)(2,1)S(1)} %held.5), channel_id=1, source_target_pairs={{0,8},{8,16},{16,24},{24,32},{32,40},{40,48},{48,56},{56,64},{64,7... | collective-permute-start | bytes 786440 | tf_op jit(solution)/shard_map/ppermute | solution.py:26
  9.3 0.0 copy-done
  9.3 0.1 fusion.near_ref
  9.4 3.2 %attend_own.1 = (f32[8,136,512]{2,1,0:T(8,128)S(1)}, f32[8,128]{1,0:T(8,128)S(1)}) custom-call(bf16[8,128,512]{2,1,0:T(8,128)(2,1)S(1)} %copy.19.qt_ref.after_ref, s32[24,128]{1,0:T(8,128)S(1)} %fusion.near_ref, bf16[1024,128]{1,0:T(8,128)(2,1)S(1)} %pad_maximum_fusion.kv_ref.value_ref), custom_call_target="tpu_custom_call" | custom-call | flops 1000 | tf_op jit(solution)/shard_map/attend_own/pallas_call | solution.py:174
  12.5 6.8 %collective-permute-done.value_ref.refs_0_ = bf16[1024,128]{1,0:T(8,128)(2,1)S(1)} collective-permute-done((bf16[1024,128]{1,0:T(8,128)(2,1)S(1)}, bf16[1024,128]{1,0:T(8,128)(2,1)S(1)}, u32[]{:S(2)}, u32[]{:S(2)}) %collective-permute-start) | collective-permute-done | bytes 262176 | tf_op jit(solution)/shard_map/ppermute | solution.py:26
  19.4 1.9 %collective-permute-start.1 = (bf16[1024,128]{1,0:T(8,128)(2,1)S(1)}, bf16[1024,128]{1,0:T(8,128)(2,1)S(1)}, u32[]{:S(2)}, u32[]{:S(2)}) collective-permute-start(bf16[1024,128]{1,0:T(8,128)(2,1)S(1)} %held.4), channel_id=1, source_target_pairs={{0,16},{8,24},{16,32},{24,40},{32,48},{40,56},{48,64},{56,72},{64,... | collective-permute-start | bytes 786440 | tf_op jit(solution)/shard_map/ppermute | solution.py:26
  21.3 0.0 collective-permute-done.2.refs_1_
  21.3 2.6 %attend_earlier.3 = (f32[8,136,512]{2,1,0:T(8,128)S(1)}, f32[8,128]{1,0:T(8,128)S(1)}) custom-call(bf16[8,128,512]{2,1,0:T(8,128)(2,1)S(1)} %copy.19.qt_ref.after_ref, bf16[1024,128]{1,0:T(8,128)(2,1)S(1)} %collective-permute-done.value_ref.refs_0_, bf16[1024,128]{1,0:T(8,128)(2,1)S(1)} %collective-permute-done.2.refs_1_, ...), custom_call_target="tpu_custom_call", output_to_operand_aliasing={{0}: (3, {})} | custom-call | flops 1000 | tf_op jit(solution)/shard_map/attend_earlier/pallas_call | solution.py:202
  23.9 1.9 %collective-permute-start.4 = (bf16[1024,128]{1,0:T(8,128)(2,1)S(1)}, bf16[1024,128]{1,0:T(8,128)(2,1)S(1)}, u32[]{:S(2)}, u32[]{:S(2)}) collective-permute-start(bf16[1024,128]{1,0:T(8,128)(2,1)S(1)} %held.7), channel_id=1, source_target_pairs={{0,8},{8,16},{16,24},{24,32},{32,40},{40,48},{48,56},{56,64},{64,7... | collective-permute-start | bytes 786440 | tf_op jit(solution)/shard_map/ppermute | solution.py:26
  25.9 4.2 %collective-permute-done.1.value_ref.refs_0_ = bf16[1024,128]{1,0:T(8,128)(2,1)S(1)} collective-permute-done((bf16[1024,128]{1,0:T(8,128)(2,1)S(1)}, bf16[1024,128]{1,0:T(8,128)(2,1)S(1)}, u32[]{:S(2)}, u32[]{:S(2)}) %collective-permute-start.1) | collective-permute-done | bytes 262176 | tf_op jit(solution)/shard_map/ppermute | solution.py:26
  30.0 1.9 %collective-permute-start.3 = (bf16[1024,128]{1,0:T(8,128)(2,1)S(1)}, bf16[1024,128]{1,0:T(8,128)(2,1)S(1)}, u32[]{:S(2)}, u32[]{:S(2)}) collective-permute-start(bf16[1024,128]{1,0:T(8,128)(2,1)S(1)} %held.6), channel_id=1, source_target_pairs={{0,8},{8,16},{16,24},{24,32},{32,40},{40,48},{48,56},{56,64},{64,7... | collective-permute-start | bytes 786440 | tf_op jit(solution)/shard_map/ppermute | solution.py:26
  32.0 1.8 %collective-permute-done.4.refs_1_ = bf16[1024,128]{1,0:T(8,128)(2,1)S(1)} collective-permute-done((bf16[1024,128]{1,0:T(8,128)(2,1)S(1)}, bf16[1024,128]{1,0:T(8,128)(2,1)S(1)}, u32[]{:S(2)}, u32[]{:S(2)}) %collective-permute-start.4) | collective-permute-done | bytes 262176 | tf_op jit(solution)/shard_map/ppermute | solution.py:26
  33.7 3.0 %attend_earlier.4 = (f32[8,136,512]{2,1,0:T(8,128)S(1)}, f32[8,128]{1,0:T(8,128)}) custom-call(bf16[8,128,512]{2,1,0:T(8,128)(2,1)S(1)} %copy.19.qt_ref.after_ref, bf16[1024,128]{1,0:T(8,128)(2,1)S(1)} %collective-permute-done.1.value_ref.refs_0_, bf16[1024,128]{1,0:T(8,128)(2,1)S(1)} %collective-permute-done.4.refs_1_, ...), custom_call_target="tpu_custom_call", output_to_operand_aliasing={{0}: (3, {})} | custom-call | flops 1000 | tf_op jit(solution)/shard_map/attend_earlier/pallas_call | solution.py:202
  36.8 3.1 %collective-permute-done.3.refs_0_ = bf16[1024,128]{1,0:T(8,128)(2,1)S(1)} collective-permute-done((bf16[1024,128]{1,0:T(8,128)(2,1)S(1)}, bf16[1024,128]{1,0:T(8,128)(2,1)S(1)}, u32[]{:S(2)}, u32[]{:S(2)}) %collective-permute-start.3) | collective-permute-done | bytes 262176 | tf_op jit(solution)/shard_map/ppermute | solution.py:26
  39.8 2.0 %attend_earlier.5 = bf16[8,64,1024]{2,1,0:T(8,128)(2,1)S(1)} custom-call(bf16[8,128,512]{2,1,0:T(8,128)(2,1)S(1)} %copy.19.qt_ref.after_ref, bf16[1024,128]{1,0:T(8,128)(2,1)S(1)} %collective-permute-done.3.refs_0_, f32[8,136,512]{2,1,0:T(8,128)S(1)} %get-tuple-element.14.refs_1_), custom_call_target="tpu_custom_call" | custom-call | flops 1000 | tf_op jit(solution)/shard_map/attend_earlier/pallas_call | solution.py:202
  41.9 28.8 %all_to_all.5 = bf16[8,64,1024]{2,1,0:T(8,128)(2,1)S(1)} all-to-all(bf16[8,64,1024]{2,1,0:T(8,128)(2,1)S(1)} %attend_earlier.5), channel_id=1, replica_groups=mesh['ctx'=64,'kvh'=8] {'kvh'}, dimensions={0} | all-to-all | bytes 2097152 | tf_op jit(solution)/shard_map/all_to_all | solution.py:257
  70.7 1.1 %copy.21 = bf16[8,8,8,1024]{3,2,0,1:T(8,128)(2,1)} copy(bf16[8,8,8,1024]{3,2,1,0:T(8,128)(2,1)S(1)} %bitcast.11) | data formatting | bytes 2097152 | tf_op jit(solution)/shard_map/reshape | solution.py:258
  (4 shorter events, 0.1 us)
Async XLA Ops:
  1.0 18.3 %collective-permute-start = (bf16[1024,128]{1,0:T(8,128)(2,1)S(1)}, bf16[1024,128]{1,0:T(8,128)(2,1)S(1)}, u32[]{:S(2)}, u32[]{:S(2)}) collective-permute-start(bf16[1024,128]{1,0:T(8,128)(2,1)S(1)} %pad_maximum_fusion.kv_ref.value_ref), channel_id=1, source_target_pairs={{0,16},{8,24},{16,32},{24,40},{32,48},{40,56},{48,64},{56,72},{64,... | collective-permute-start | bytes 786440 | tf_op jit(solution)/shard_map/ppermute | solution.py:26
  6.8 2.5 %copy-start = (s32[32768]{0:T(1024)S(1)}, s32[32768]{0:T(1024)}, u32[]{:S(2)}) copy-start(s32[32768]{0:T(1024)} %param.7) | copy-start | bytes 393220
  7.4 13.9 %collective-permute-start.2 = (bf16[1024,128]{1,0:T(8,128)(2,1)S(1)}, bf16[1024,128]{1,0:T(8,128)(2,1)S(1)}, u32[]{:S(2)}, u32[]{:S(2)}) collective-permute-start(bf16[1024,128]{1,0:T(8,128)(2,1)S(1)} %held.5), channel_id=1, source_target_pairs={{0,8},{8,16},{16,24},{24,32},{32,40},{40,48},{48,56},{56,64},{64,7... | collective-permute-start | bytes 786440 | tf_op jit(solution)/shard_map/ppermute | solution.py:26
  19.4 10.7 %collective-permute-start.1 = (bf16[1024,128]{1,0:T(8,128)(2,1)S(1)}, bf16[1024,128]{1,0:T(8,128)(2,1)S(1)}, u32[]{:S(2)}, u32[]{:S(2)}) collective-permute-start(bf16[1024,128]{1,0:T(8,128)(2,1)S(1)} %held.4), channel_id=1, source_target_pairs={{0,16},{8,24},{16,32},{24,40},{32,48},{40,56},{48,64},{56,72},{64,... | collective-permute-start | bytes 786440 | tf_op jit(solution)/shard_map/ppermute | solution.py:26
  23.9 9.8 %collective-permute-start.4 = (bf16[1024,128]{1,0:T(8,128)(2,1)S(1)}, bf16[1024,128]{1,0:T(8,128)(2,1)S(1)}, u32[]{:S(2)}, u32[]{:S(2)}) collective-permute-start(bf16[1024,128]{1,0:T(8,128)(2,1)S(1)} %held.7), channel_id=1, source_target_pairs={{0,8},{8,16},{16,24},{24,32},{32,40},{40,48},{48,56},{56,64},{64,7... | collective-permute-start | bytes 786440 | tf_op jit(solution)/shard_map/ppermute | solution.py:26
  30.0 9.8 %collective-permute-start.3 = (bf16[1024,128]{1,0:T(8,128)(2,1)S(1)}, bf16[1024,128]{1,0:T(8,128)(2,1)S(1)}, u32[]{:S(2)}, u32[]{:S(2)}) collective-permute-start(bf16[1024,128]{1,0:T(8,128)(2,1)S(1)} %held.6), channel_id=1, source_target_pairs={{0,8},{8,16},{16,24},{24,32},{32,40},{40,48},{48,56},{56,64},{64,7... | collective-permute-start | bytes 786440 | tf_op jit(solution)/shard_map/ppermute | solution.py:26
